TPU v7x, 32 devices: a whole 2x2x4 slice. The times are simulated.
32 devices in a mesh: groups: 2 (over y), wide: 4 (over z), narrow: 4 (over x, core).
Axes of the slice: x: 2, y: 2, z: 4, core: 2. Of those that a mesh axis runs over, the one named last changes fastest.
Arguments:
- picture_vectors: bfloat16 [512, 768], P(('groups', 'wide', 'narrow')), parts along dimension 0, may hold values from -0.24 to 0.24
- caption_vectors: bfloat16 [512, 768], P(('groups', 'wide', 'narrow')), parts along dimension 0, may hold values from -0.24 to 0.24
- matching_caption_index: int32 [512], P(('groups', 'wide', 'narrow')), parts along dimension 0, may hold values from 0 to 255, as said below
- sharpness_array: float32 [1], replicated, may hold values from 5 to 15
- offset_term: float32 [1], replicated, may hold values from -6 to -3
Outputs:
- image_grad: float32 [512, 768], P(('groups', 'wide', 'narrow')), parts along dimension 0
- text_grad: float32 [512, 768], P(('groups', 'wide', 'narrow')), parts along dimension 0
- summary_outputs: float32 [6], P('groups'), parts along dimension 0
There are 2 independent parts, one for each index of `groups`. A program takes and returns all parts, laid end to end along the dimension named above; an argument that names none is the same for every part. Nothing has to cross between parts.
Inputs may be any that keep to these rules, and one draw needn't show every extreme that they name: `matching_caption_index`: partner is a permutation of the 256 text indices of the group.
All inputs are finite; a program needn't handle non-finite values.
Results may differ from a plain program's by a relative error of at most 0.00082.
Values may be sent and summed in bfloat16 or wider, within the bound.
No kernel may reach another device: no remote copies, remote signals or barrier semaphores. Data moves between devices by JAX's collectives and lax.ppermute only.
A program may use at most 64 MiB of HBM per device.

v0:
```python
import jax
import jax.numpy as jnp
from jax import lax
from jax.sharding import PartitionSpec as P


def normalize(rows):
    values = rows.astype(jnp.float32)
    scales = lax.rsqrt(jnp.sum(values * values, axis=1, keepdims=True) + 1e-06)
    return (values * scales, scales)


def backnorm(unit, scales, grad_unit):
    return scales * (grad_unit - unit * jnp.sum(unit * grad_unit, axis=1, keepdims=True))


def per_device(
    picture_vectors, caption_vectors, matching_caption_index, sharpness_array, offset_term
):
    local_rows = picture_vectors.shape[0]
    narrow_device_count = lax.axis_size("narrow")
    wide_count = lax.axis_size("wide")
    narrow_index = lax.axis_index("narrow")
    sharpness_factor = sharpness_array[0]
    shift = offset_term[0]
    unit_img, inv_img = normalize(picture_vectors)
    normalized_text_rows, inv_txt = normalize(caption_vectors)
    img_half = unit_img.astype(jnp.bfloat16)
    txt_half = normalized_text_rows.astype(jnp.bfloat16)
    img_block, mates = (
        lax.all_gather(img_half, "narrow", axis=0, tiled=True),
        lax.all_gather(matching_caption_index, "narrow", axis=0, tiled=True),
    )
    txt_column = lax.all_gather(txt_half, "wide", axis=0, tiled=True)
    offsets = jnp.arange(txt_column.shape[0], dtype=jnp.int32)
    columns = (
        offsets // local_rows * narrow_device_count + narrow_index
    ) * local_rows + offsets % local_rows
    cosine = jnp.dot(img_block, txt_column.T, preferred_element_type=jnp.float32)
    logit = sharpness_factor * cosine + shift
    sign = jnp.where(mates[:, None] == columns[None, :], 1.0, -1.0).astype(jnp.float32)
    loss_part = jnp.sum(jax.nn.softplus(-sign * logit))
    slope = -sign * jax.nn.sigmoid(-sign * logit)
    temp_part = jnp.sum(slope * cosine)
    bias_part = jnp.sum(slope)
    weighted = (sharpness_factor * slope).astype(jnp.bfloat16)
    img_part = jnp.dot(weighted, txt_column, preferred_element_type=jnp.float32)
    text_share = lax.dot_general(
        weighted, img_block, (((0,), (0,)), ((), ())), preferred_element_type=jnp.float32
    )
    caption_derivative_on_sphere = lax.psum_scatter(
        text_share, "wide", scatter_dimension=0, tiled=True
    )
    img_grad_unit = lax.psum_scatter(img_part, "narrow", scatter_dimension=0, tiled=True)
    loss_all, temp_all, bias_all = lax.psum((loss_part, temp_part, bias_part), ("wide", "narrow"))
    image_text_pair_count = local_rows * wide_count * narrow_device_count
    summary_outputs = jnp.stack([loss_all / image_text_pair_count, temp_all, bias_all])
    image_grad = backnorm(unit_img, inv_img, img_grad_unit)
    text_grad = backnorm(normalized_text_rows, inv_txt, caption_derivative_on_sphere)
    return (image_grad, text_grad, summary_outputs)


def solution(mesh):
    placed = (
        P(("groups", "wide", "narrow"), None),
        P(("groups", "wide", "narrow"), None),
        P(("groups", "wide", "narrow")),
        P(),
        P(),
    )
    return jax.shard_map(
        per_device,
        mesh=mesh,
        in_specs=placed,
        out_specs=(
            P(("groups", "wide", "narrow"), None),
            P(("groups", "wide", "narrow"), None),
            P("groups"),
        ),
        check_vma=False,
    )
```

profile of v0, /device:TPU:0, one launch (start us, length us, event | category | flops | bytes accessed | tf_op | source)
XLA Modules:
  0.0 89.3 jit_solution(6638815900601545978)
XLA Ops:
  7.2 0.0 copy-start
  7.2 0.0 reduce-scatter.5.cloned.1.call-start
  8.5 0.9 fusion.9
  9.4 0.0 copy-done
  9.4 0.1 fusion.13
  9.5 0.0 copy-start.5
  9.5 0.6 copy-done.5
  10.2 0.6 dynamic-slice
  11.4 0.0 copy-start.4
  11.4 0.6 copy-done.4
  12.1 0.2 dynamic-update-slice
  12.3 6.3 %all-reduce = s32[64]{0:T(128)S(1)} all-reduce(s32[64]{0:T(128)S(1)} %dynamic-update-slice), channel_id=1, replica_groups=mesh['groups'=2,'wide'=4,'narrow'=4] {'narrow'}, use_global_device_ids=true, to_apply=%add | all-reduce | flops 64 | bytes 512
  18.6 0.0 copy-start.1
  18.6 0.1 fusion.2
  18.7 0.7 copy-done.1
  19.3 0.1 fusion.5
  19.4 5.3 %all_gather.10 = bf16[64,768]{1,0:T(8,128)(2,1)S(1)} all-gather(bf16[16,768]{1,0:T(8,128)(2,1)S(1)} %fusion.5), channel_id=1, replica_groups=mesh['groups'=2,'wide'=4,'narrow'=4] {'narrow'}, dimensions={0}, use_global_device_ids=true | all-gather | bytes 122880 | tf_op jit(solution)/shard_map/all_gather | solution.py:31
  24.7 13.4 %all_gather.11 = bf16[64,768]{1,0:T(8,128)(2,1)S(1)} all-gather(bf16[16,768]{1,0:T(8,128)(2,1)S(1)} %fusion.2), channel_id=1, replica_groups=mesh['groups'=2,'wide'=4,'narrow'=4] {'wide'}, dimensions={0}, use_global_device_ids=true | all-gather | bytes 122880 | tf_op jit(solution)/shard_map/all_gather | solution.py:34
  38.2 0.8 fusion.14
  39.0 1.0 %fusion.15 = f32[64,768]{1,0:T(8,128)} fusion(bf16[64,768]{1,0:T(8,128)(2,1)S(1)} %all_gather.10, f32[]{:T(128)} %bitcast.10, f32[64,64]{1,0:T(8,128)S(1)} %get-tuple-element.9, f32[]{:T(128)} %bitcast.15, s32[64]{0:T(128)S(1)} %fusion.17, s32[64]{0:T(128)S(1)} %all-reduce), kind=kOutput, calls=%fused_computation.25 | convolution fusion | flops 6340608 | bytes 311816 | tf_op jit(solution)/shard_map/dot_general | solution.py:48
  40.0 0.0 reduce-scatter.5.cloned.1.call-update
  40.0 0.0 reduce-scatter.3.cloned.1.call-start
  40.1 0.9 %fusion.16 = f32[64,768]{1,0:T(8,128)} fusion(bf16[64,768]{1,0:T(8,128)(2,1)S(1)} %all_gather.11, f32[]{:T(128)} %bitcast.12, f32[64,64]{1,0:T(8,128)S(1)} %get-tuple-element.9, f32[]{:T(128)} %bitcast.13, s32[64]{0:T(128)S(1)} %fusion.17, s32[64]{0:T(128)S(1)} %all-reduce), kind=kOutput, calls=%fused_computation.26 | convolution fusion | flops 6340608 | bytes 311816 | tf_op jit(solution)/shard_map/dot_general | solution.py:47
  41.0 0.0 reduce-scatter.3.cloned.1.call-update
  41.0 31.1 %all-reduce.1 = (f32[1]{0:T(128)}, f32[1]{0:T(128)}, f32[]{:T(128)}) all-reduce(f32[1]{0:T(128)} %bitcast.5, f32[1]{0:T(128)} %bitcast.4, f32[]{:T(128)} %get-tuple-element.3), channel_id=1, replica_groups=mesh['groups'=2,'wide'=4,'narrow'=4] {'wide','narrow'}, use_global_device_ids=true, to_apply=%region_11.12 | all-reduce | flops 3 | bytes 24 | tf_op jit(solution)/shard_map/psum | solution.py:55
  72.8 1.9 %pad_maximum_fusion = f32[3]{0:T(128)} fusion(f32[1]{0:T(128)} %get-tuple-element.6, f32[1]{0:T(128)} %get-tuple-element.7, f32[1]{0:T(128)} %bitcast.3), kind=kLoop, calls=%fused_computation.36 | loop fusion | flops 6 | bytes 24 | tf_op jit(solution)/shard_map/stack | solution.py:57
  74.7 0.0 reduce-scatter.5.cloned.1.call-done
  74.7 0.0 copy-start.2
  74.7 1.1 %fusion.10 = f32[16]{0:T(128)S(1)} fusion(f32[16,768]{1,0:T(8,128)} %reduce-scatter.5.cloned.1.call-done, bf16[16,768]{1,0:T(8,128)(2,1)S(1)} %copy-done, f32[16]{0:T(128)S(1)} %add_rsqrt_fusion), kind=kLoop, calls=%fused_computation.15 | loop fusion | flops 49136 | bytes 73856 | tf_op jit(solution)/shard_map/reduce_sum | solution.py:14
  75.8 0.0 copy-done.2
  75.8 0.7 fusion.12
  76.5 4.2 %reduce-scatter.3.cloned.1.call-done = f32[16,768]{1,0:T(8,128)} async-done(((f32[64,768]{1,0:T(8,128)}), f32[16,768]{1,0:T(8,128)}) %reduce-scatter.3.cloned.1.call-update) | async-done | bytes 49168 | tf_op jit(solution)/shard_map/reduce_scatter | solution.py:54
  80.7 0.0 copy-start.3
  80.7 1.1 %fusion.6 = f32[16]{0:T(128)S(1)} fusion(f32[16,768]{1,0:T(8,128)} %reduce-scatter.3.cloned.1.call-done, bf16[16,768]{1,0:T(8,128)(2,1)S(1)} %copy-done.1, f32[16]{0:T(128)S(1)} %add_rsqrt_fusion.1), kind=kLoop, calls=%fused_computation.11 | loop fusion | flops 49136 | bytes 73856 | tf_op jit(solution)/shard_map/reduce_sum | solution.py:14
  81.7 0.0 copy-done.3
  81.7 0.7 fusion.8
  (4 shorter events, 0.0 us)
Async XLA Ops:
  7.2 2.2 %copy-start = (bf16[16,768]{1,0:T(8,128)(2,1)S(1)}, bf16[16,768]{1,0:T(8,128)(2,1)}, u32[]{:S(2)}) copy-start(bf16[16,768]{1,0:T(8,128)(2,1)} %param.6) | copy-start | bytes 73732
  7.2 67.6 %reduce-scatter.5.cloned.1.call-start = ((), (), s32[]{:S(2)}) async-start(), calls=%async_computation.3 | async-start | bytes 245760 | tf_op jit(solution)/shard_map/reduce_scatter | solution.py:51
  9.5 0.7 copy-start.5
  11.4 0.7 copy-start.4
  18.6 0.7 copy-start.1
  40.0 40.6 %reduce-scatter.3.cloned.1.call-start = ((), (), s32[]{:S(2)}) async-start(), calls=%async_computation.2 | async-start | bytes 245760 | tf_op jit(solution)/shard_map/reduce_scatter | solution.py:54
  74.7 1.1 %copy-start.2 = (f32[16,768]{1,0:T(8,128)S(1)}, f32[16,768]{1,0:T(8,128)}, u32[]{:S(2)}) copy-start(f32[16,768]{1,0:T(8,128)} %reduce-scatter.5.cloned.1.call-done) | copy-start | bytes 147460
  80.7 1.1 %copy-start.3 = (f32[16,768]{1,0:T(8,128)S(1)}, f32[16,768]{1,0:T(8,128)}, u32[]{:S(2)}) copy-start(f32[16,768]{1,0:T(8,128)} %reduce-scatter.3.cloned.1.call-done) | copy-start | bytes 147460
Sparse Core Ops, SparseCore 0:
  40.2 19.8 reduce-scatter.4
  62.6 17.9 reduce-scatter.2
where the time goes:
time: 89.8 us; the launch traced here: 89.3 us
  blocking collectives  56.2 us (63%)
  between operations  16.7 us (19%)
  other arithmetic  6.58 us (7%)
  waiting for transfers between devices  4.19 us (5%)
  matrix products  2.73 us (3%)
  local copies, waits for them, and re-layouts  2.72 us (3%)
    psum x1, blocking collectives, per_device(): lax.psum((loss_part, temp_part, bias_part), ('wide', 'narrow'))  31.1 us
    all_gather x1, blocking collectives, per_device(): txt_column = lax.all_gather(txt_half, 'wide', axis=0, tiled=True)  13.4 us
    unnamed x1, blocking collectives  6.35 us
    all_gather x1, blocking collectives, per_device(): lax.all_gather(img_half, 'narrow', axis=0, tiled=True)  5.32 us
    reduce_scatter x1, waiting for transfers between devices, per_device(): lax.psum_scatter(img_part, 'narrow', scatter_dimension=0, tiled=True)  4.16 us
    unnamed x15, local copies, waits for them, and re-layouts  2.72 us
    reduce_sum x2, other arithmetic, backnorm(): jnp.sum(unit * grad_unit, axis=1, keepdims=True)  2.11 us
    another operation x1, other arithmetic, per_device(): jnp.stack([loss_all / image_text_pair_count, temp_all, bias_all])  1.92 us
  transfers between devices with their start and end apart: 2, of which 1 were waited for; matrix products, arithmetic and copies ran while one was open for 5% of the time, Pallas kernels for 0%

commit v1 on v0

v1 whole, which is shorter than its diff:
```python
import jax
import jax.numpy as jnp
from jax import lax
from jax.experimental import pallas as pl
from jax.experimental.pallas import tpu as pltpu
from jax.sharding import PartitionSpec as P

GROUP = ("wide", "narrow")
LANES = 128
VMEM = pl.BlockSpec(memory_space=pltpu.VMEM)
SMEM = pl.BlockSpec(memory_space=pltpu.SMEM)


def normalize(rows):
    values = rows.astype(jnp.float32)
    scales = lax.rsqrt(jnp.sum(values * values, axis=1, keepdims=True) + 1e-06)
    return (values * scales, scales)


def backnorm(unit, scales, grad_unit):
    return scales * (grad_unit - unit * jnp.sum(unit * grad_unit, axis=1, keepdims=True))


def pair_terms(cosine, logit, matched):
    against = jnp.where(matched, -logit, logit)
    small = jnp.exp(-jnp.abs(logit))
    loss = jnp.maximum(against, 0.0) + jnp.log1p(small)
    sigma = jnp.where(against >= 0.0, 1.0, small) / (1.0 + small)
    return loss, jnp.where(matched, -sigma, sigma)


def pack_kernel(mates_ref, img_ref, txt_ref, out_ref):
    rows, width = img_ref.shape
    tiles = width // LANES
    for t in range(tiles):
        out_ref[t] = img_ref[:, t * LANES : (t + 1) * LANES]
        out_ref[tiles + t] = txt_ref[:, t * LANES : (t + 1) * LANES]
    row = lax.broadcasted_iota(jnp.int32, (rows, LANES), 0)
    mates = jnp.zeros((rows, LANES), jnp.int32)
    for r in range(rows):
        mates = jnp.where(row == r, mates_ref[r], mates)
    out_ref[2 * tiles] = mates.astype(jnp.float32).astype(jnp.bfloat16)


def pair_kernel(distances, narrow, sharp_ref, shift_ref, *refs):
    blocks = refs[: len(distances)]
    image_out, text_out, summary_out, img_half, txt_half, mates, weights = refs[len(distances) :]
    count = len(distances)
    rows, width = image_out.shape
    tiles = width // LANES
    total = rows * count
    me = lax.axis_index("wide") * narrow + lax.axis_index("narrow")
    sharp, shift = sharp_ref[0], shift_ref[0]

    def unit_tiles(block, first):
        values = [block[first + t].astype(jnp.float32) for t in range(tiles)]
        squares = values[0] * values[0]
        for v in values[1:]:
            squares = squares + v * v
        scales = lax.rsqrt(jnp.sum(squares, axis=1, keepdims=True) + 1e-06)
        return [v * scales for v in values], scales

    own = None
    for distance, block in zip(distances, blocks):
        here = pl.ds(pl.multiple_of((me ^ distance) * rows, rows), rows)
        img_units, img_scale = unit_tiles(block, 0)
        txt_units, txt_scale = unit_tiles(block, tiles)
        for t in range(tiles):
            lanes = slice(t * LANES, (t + 1) * LANES)
            img_half[here, lanes] = img_units[t].astype(jnp.bfloat16)
            txt_half[here, lanes] = txt_units[t].astype(jnp.bfloat16)
        mates[here, :] = block[2 * tiles].astype(jnp.float32)
        if distance == 0:
            own = (img_units, img_scale, txt_units, txt_scale)

    nt = (((1,), (1,)), ((), ()))
    cosine = lax.dot_general(img_half[...], txt_half[...], nt, preferred_element_type=jnp.float32)
    logit = sharp * cosine + shift
    column = lax.broadcasted_iota(jnp.int32, (total, LANES), 1).astype(jnp.float32)
    matched = jnp.concatenate(
        [mates[...] == column + float(c * LANES) for c in range(total // LANES)], axis=1
    )
    loss, slope = pair_terms(cosine, logit, matched)
    summary_out[0] = jnp.sum(loss) / total
    summary_out[1] = jnp.sum(slope * cosine)
    summary_out[2] = jnp.sum(slope)
    weights[...] = (sharp * slope).astype(jnp.bfloat16)

    mine = pl.ds(pl.multiple_of(me * rows, rows), rows)
    picked = (
        lax.broadcasted_iota(jnp.int32, (rows, total), 1)
        == lax.broadcasted_iota(jnp.int32, (rows, total), 0) + me * rows
    )
    text_weights = lax.dot_general(
        picked.astype(jnp.float32).astype(jnp.bfloat16),
        weights[...],
        nt,
        preferred_element_type=jnp.float32,
    ).astype(jnp.bfloat16)
    img_grad = jnp.dot(weights[mine, :], txt_half[...], preferred_element_type=jnp.float32)
    txt_grad = jnp.dot(text_weights, img_half[...], preferred_element_type=jnp.float32)

    def store(out, units, scale, grad):
        parts = [grad[:, t * LANES : (t + 1) * LANES] for t in range(tiles)]
        along = units[0] * parts[0]
        for u, g in zip(units[1:], parts[1:]):
            along = along + u * g
        along = jnp.sum(along, axis=1, keepdims=True)
        for t in range(tiles):
            out[:, t * LANES : (t + 1) * LANES] = scale * (parts[t] - units[t] * along)

    store(image_out, own[0], own[1], img_grad)
    store(text_out, own[2], own[3], txt_grad)


def small_group(wide, narrow, images, texts, mates, sharpness, offset):
    rows, width = images.shape
    count = wide * narrow
    tiles = 2 * (width // LANES) + 1
    packed = pl.pallas_call(
        pack_kernel,
        out_shape=jax.ShapeDtypeStruct((tiles, rows, LANES), jnp.bfloat16),
        in_specs=[SMEM, VMEM, VMEM],
        out_specs=VMEM,
    )(mates, images, texts)

    def swap(x, distance):
        return lax.ppermute(x, GROUP, [(i, i ^ distance) for i in range(count)])

    held = {0: packed}
    bit = narrow
    held[2 * bit] = swap(packed, 2 * bit)
    held[bit] = swap(packed, bit)
    held[3 * bit] = swap(held[2 * bit], bit)
    for bit in (2, 1):
        for distance in list(held):
            held[distance + bit] = swap(held[distance], bit)

    distances = tuple(held)
    total = rows * count
    kernel = lambda *refs: pair_kernel(distances, narrow, *refs)
    return pl.pallas_call(
        kernel,
        out_shape=(
            jax.ShapeDtypeStruct((rows, width), jnp.float32),
            jax.ShapeDtypeStruct((rows, width), jnp.float32),
            jax.ShapeDtypeStruct((3,), jnp.float32),
        ),
        in_specs=[SMEM, SMEM] + [VMEM] * count,
        out_specs=(VMEM, VMEM, SMEM),
        scratch_shapes=[
            pltpu.VMEM((total, width), jnp.bfloat16),
            pltpu.VMEM((total, width), jnp.bfloat16),
            pltpu.VMEM((total, LANES), jnp.float32),
            pltpu.VMEM((total, total), jnp.bfloat16),
        ],
        compiler_params=pltpu.CompilerParams(vmem_limit_bytes=32 * 1024 * 1024),
    )(sharpness, offset, *held.values())


def any_group(wide, narrow, images, texts, mates, sharpness, offset):
    rows = images.shape[0]
    total = rows * wide * narrow
    first = (lax.axis_index("wide") * narrow + lax.axis_index("narrow")) * rows
    unit_img, inv_img = normalize(images)
    unit_txt, inv_txt = normalize(texts)
    img_half, txt_half = unit_img.astype(jnp.bfloat16), unit_txt.astype(jnp.bfloat16)
    all_img = lax.all_gather(img_half, GROUP, axis=0, tiled=True)
    all_txt = lax.all_gather(txt_half, GROUP, axis=0, tiled=True)
    all_mates = lax.all_gather(mates, GROUP, axis=0, tiled=True)
    sharp, shift = sharpness[0], offset[0]

    def weigh(cosine, matched):
        loss, slope = pair_terms(cosine, sharp * cosine + shift, matched)
        return loss, slope, (sharp * slope).astype(jnp.bfloat16)

    here = first + jnp.arange(rows, dtype=jnp.int32)
    there = jnp.arange(total, dtype=jnp.int32)
    cosine = jnp.dot(img_half, all_txt.T, preferred_element_type=jnp.float32)
    loss, slope, weighted = weigh(cosine, mates[:, None] == there[None, :])
    sums = jnp.stack([jnp.sum(loss) / total, jnp.sum(slope * cosine), jnp.sum(slope)])
    img_grad = jnp.dot(weighted, all_txt, preferred_element_type=jnp.float32)
    turned = jnp.dot(txt_half, all_img.T, preferred_element_type=jnp.float32)
    weighted = weigh(turned, all_mates[None, :] == here[:, None])[2]
    txt_grad = jnp.dot(weighted, all_img, preferred_element_type=jnp.float32)
    return (
        backnorm(unit_img, inv_img, img_grad),
        backnorm(unit_txt, inv_txt, txt_grad),
        lax.psum(sums, GROUP),
    )


def solution(mesh):
    wide, narrow = mesh.shape["wide"], mesh.shape["narrow"]

    def per_device(images, texts, mates, sharpness, offset):
        total = images.shape[0] * wide * narrow
        small = wide == 4 and narrow == 4 and total <= 256 and total % LANES == 0
        form = small_group if small else any_group
        return form(wide, narrow, images, texts, mates, sharpness, offset)

    rows = P(("groups", "wide", "narrow"))
    return jax.shard_map(
        per_device,
        mesh=mesh,
        in_specs=(rows, rows, rows, P(), P()),
        out_specs=(rows, rows, P("groups")),
        check_vma=False,
    )
```

time: 89.8 us -> 22.7 us (0.25)
  blocking collectives: 56.2 us -> 0 us
  between operations: 16.7 us -> 1.99 us
  starting transfers between devices: 0.08 us -> 12 us
  other arithmetic: 6.58 us -> 0 us
  Pallas kernels: 0 us -> 3.24 us
  matrix products: 2.73 us -> 0 us
  local copies, waits for them, and re-layouts: 2.72 us -> 0.8 us
    psum x1 -> x0, blocking collectives: 31.1 us -> none  [per_device(): lax.psum((loss_part, temp_part, bias_part), ('wide', 'narrow'))]
    all_gather x2 -> x0, blocking collectives: 18.8 us -> none  [the longest x1 13.4 us: per_device(): txt_column = lax.all_gather(txt_half, 'wide', axis=0, tiled=True)]
    ppermute x0 -> x15, starting transfers between devices: none -> 12 us  [swap(): return lax.ppermute(x, GROUP, [(i, i ^ distance) for i in range(count)])]
    unnamed x1 -> x0, blocking collectives: 6.35 us -> none
    ppermute x0 -> x15, waiting for transfers between devices: none -> 4.36 us  [swap(): return lax.ppermute(x, GROUP, [(i, i ^ distance) for i in range(count)])]
    reduce_scatter x2 -> x0, waiting for transfers between devices: 4.16 us -> none  [the longest x1 4.16 us: per_device(): lax.psum_scatter(img_part, 'narrow', scatter_dimension=0, tiled=True)]
    pallas_call x0 -> x2, Pallas kernels: none -> 3.24 us  [the longest x1 1.84 us: small_group(): pl.pallas_call(kernel, out_shape=(jax.ShapeDtypeStruct((rows, width), jnp...]
    reduce_sum x4 -> x0, other arithmetic: 3.09 us -> none  [the longest x2 2.11 us: backnorm(): jnp.sum(unit * grad_unit, axis=1, keepdims=True)]
  transfers between devices with their start and end apart: 2 -> 15, of which waited for: 1 -> 4; matrix products, arithmetic and copies ran while one was open for 5% -> 0% of each run, Pallas kernels for 0% -> 0%
where the time goes in v1:
time: 22.7 us; the launch traced here: 22.4 us
  starting transfers between devices  12 us (53%)
  waiting for transfers between devices  4.36 us (19%)
  Pallas kernels  3.24 us (14%)
  between operations  1.99 us (9%)
  local copies, waits for them, and re-layouts  0.8 us (4%)
    ppermute x15, starting transfers between devices, swap(): return lax.ppermute(x, GROUP, [(i, i ^ distance) for i in range(count)])  12 us
    ppermute x15, waiting for transfers between devices, swap(): return lax.ppermute(x, GROUP, [(i, i ^ distance) for i in range(count)])  4.36 us
    pallas_call x1, Pallas kernels, small_group(): pl.pallas_call(kernel, out_shape=(jax.ShapeDtypeStruct((rows, width), jnp...  1.84 us
    pallas_call x1, Pallas kernels, small_group(): pl.pallas_call(pack_kernel, out_shape=jax.ShapeDtypeStruct((tiles, rows,...  1.4 us
    unnamed x2, local copies, waits for them, and re-layouts  0.8 us
  transfers between devices with their start and end apart: 15, of which 4 were waited for; matrix products, arithmetic and copies ran while one was open for 0% of the time, Pallas kernels for 0%

profile of v1, /device:TPU:0, one launch (start us, length us, event | category | flops | bytes accessed | tf_op | source)
XLA Modules:
  0.0 22.4 jit_solution(13698673883131764503)
XLA Ops:
  0.6 1.4 %shard_map.76.refs_2_ = bf16[13,16,128]{2,1,0:T(8,128)(2,1)} custom-call(s32[16]{0:T(128)} %mates_ref.1, bf16[16,768]{1,0:T(8,128)(2,1)} %img_ref.1, bf16[16,768]{1,0:T(8,128)(2,1)} %txt_ref.1), custom_call_target="tpu_custom_call" | custom-call | tf_op jit(solution)/shard_map/pallas_call | solution.py:120
  2.0 4.0 %collective-permute-start = (bf16[13,16,128]{2,1,0:T(8,128)(2,1)}, bf16[13,16,128]{2,1,0:T(8,128)(2,1)S(1)}, u32[]{:S(2)}, u32[]{:S(2)}) collective-permute-start(bf16[13,16,128]{2,1,0:T(8,128)(2,1)} %shard_map.76.refs_2_), channel_id=1, source_target_pairs={{0,8},{1,9},{2,10},{3,11},{4,12},{5,13},{6,14},{7,15},{8,0},{9,1},... | collective-permute-start | bytes 159752 | tf_op jit(solution)/shard_map/ppermute | solution.py:128
  6.1 1.5 %collective-permute-start.3 = (bf16[13,16,128]{2,1,0:T(8,128)(2,1)}, bf16[13,16,128]{2,1,0:T(8,128)(2,1)S(1)}, u32[]{:S(2)}, u32[]{:S(2)}) collective-permute-start(bf16[13,16,128]{2,1,0:T(8,128)(2,1)} %shard_map.76.refs_2_), channel_id=1, source_target_pairs={{0,2},{1,3},{2,0},{3,1},{4,6},{5,7},{6,4},{7,5},{8,10},{9,11},{10,... | collective-permute-start | bytes 159752 | tf_op jit(solution)/shard_map/ppermute | solution.py:128
  7.6 1.6 %collective-permute-start.1 = (bf16[13,16,128]{2,1,0:T(8,128)(2,1)}, bf16[13,16,128]{2,1,0:T(8,128)(2,1)S(1)}, u32[]{:S(2)}, u32[]{:S(2)}) collective-permute-start(bf16[13,16,128]{2,1,0:T(8,128)(2,1)} %shard_map.76.refs_2_), channel_id=1, source_target_pairs={{0,4},{1,5},{2,6},{3,7},{4,0},{5,1},{6,2},{7,3},{8,12},{9,13},{10,... | collective-permute-start | bytes 159752 | tf_op jit(solution)/shard_map/ppermute | solution.py:128
  9.1 0.0 collective-permute-start.7
  9.1 0.0 collective-permute-done.refs_3_
  9.1 1.5 %collective-permute-start.2 = (bf16[13,16,128]{2,1,0:T(8,128)(2,1)S(1)}, bf16[13,16,128]{2,1,0:T(8,128)(2,1)S(1)}, u32[]{:S(2)}, u32[]{:S(2)}) collective-permute-start(bf16[13,16,128]{2,1,0:T(8,128)(2,1)S(1)} %collective-permute-done.refs_3_), channel_id=1, source_target_pairs={{0,4},{1,5},{2,6},{3,7},{4,0},{5,1},{6,2},{7,3},{8,12},{9,13},{10,... | collective-permute-start | bytes 159752 | tf_op jit(solution)/shard_map/ppermute | solution.py:128
  10.6 0.0 collective-permute-done.3.refs_6_
  10.6 0.0 collective-permute-start.11
  10.6 1.3 %collective-permute-done.1.refs_4_ = bf16[13,16,128]{2,1,0:T(8,128)(2,1)S(1)} collective-permute-done((bf16[13,16,128]{2,1,0:T(8,128)(2,1)}, bf16[13,16,128]{2,1,0:T(8,128)(2,1)S(1)}, u32[]{:S(2)}, u32[]{:S(2)}) %collective-permute-start.1) | collective-permute-done | bytes 53280 | tf_op jit(solution)/shard_map/ppermute | solution.py:128
  11.9 0.0 collective-permute-start.9
  11.9 0.5 %collective-permute-start.5 = (bf16[13,16,128]{2,1,0:T(8,128)(2,1)S(1)}, bf16[13,16,128]{2,1,0:T(8,128)(2,1)S(1)}, u32[]{:S(2)}, u32[]{:S(2)}) collective-permute-start(bf16[13,16,128]{2,1,0:T(8,128)(2,1)S(1)} %collective-permute-done.1.refs_4_), channel_id=1, source_target_pairs={{0,2},{1,3},{2,0},{3,1},{4,6},{5,7},{6,4},{7,5},{8,10},{9,11},{10,... | collective-permute-start | bytes 159752 | tf_op jit(solution)/shard_map/ppermute | solution.py:128
  12.4 0.0 collective-permute-done.7.refs_10_
  12.4 1.5 %collective-permute-start.4 = (bf16[13,16,128]{2,1,0:T(8,128)(2,1)S(1)}, bf16[13,16,128]{2,1,0:T(8,128)(2,1)S(1)}, u32[]{:S(2)}, u32[]{:S(2)}) collective-permute-start(bf16[13,16,128]{2,1,0:T(8,128)(2,1)S(1)} %collective-permute-done.refs_3_), channel_id=1, source_target_pairs={{0,2},{1,3},{2,0},{3,1},{4,6},{5,7},{6,4},{7,5},{8,10},{9,11},{10,... | collective-permute-start | bytes 159752 | tf_op jit(solution)/shard_map/ppermute | solution.py:128
  13.9 0.0 collective-permute-done.2.refs_5_
  13.9 0.9 %collective-permute-start.6 = (bf16[13,16,128]{2,1,0:T(8,128)(2,1)S(1)}, bf16[13,16,128]{2,1,0:T(8,128)(2,1)S(1)}, u32[]{:S(2)}, u32[]{:S(2)}) collective-permute-start(bf16[13,16,128]{2,1,0:T(8,128)(2,1)S(1)} %collective-permute-done.2.refs_5_), channel_id=1, source_target_pairs={{0,2},{1,3},{2,0},{3,1},{4,6},{5,7},{6,4},{7,5},{8,10},{9,11},{10,... | collective-permute-start | bytes 159752 | tf_op jit(solution)/shard_map/ppermute | solution.py:128
  14.8 0.0 collective-permute-done.11.refs_14_
  14.9 0.0 collective-permute-start.8
  14.9 0.0 collective-permute-done.9.refs_12_
  14.9 0.5 %collective-permute-start.10 = (bf16[13,16,128]{2,1,0:T(8,128)(2,1)S(1)}, bf16[13,16,128]{2,1,0:T(8,128)(2,1)S(1)}, u32[]{:S(2)}, u32[]{:S(2)}) collective-permute-start(bf16[13,16,128]{2,1,0:T(8,128)(2,1)S(1)} %collective-permute-done.2.refs_5_), channel_id=1, source_target_pairs={{0,1},{1,0},{2,3},{3,2},{4,5},{5,4},{6,7},{7,6},{8,9},{9,8},{10,11... | collective-permute-start | bytes 159752 | tf_op jit(solution)/shard_map/ppermute | solution.py:128
  15.4 1.2 %collective-permute-done.5.refs_8_ = bf16[13,16,128]{2,1,0:T(8,128)(2,1)S(1)} collective-permute-done((bf16[13,16,128]{2,1,0:T(8,128)(2,1)S(1)}, bf16[13,16,128]{2,1,0:T(8,128)(2,1)S(1)}, u32[]{:S(2)}, u32[]{:S(2)}) %collective-permute-start.5) | collective-permute-done | bytes 53280 | tf_op jit(solution)/shard_map/ppermute | solution.py:128
  16.5 0.0 collective-permute-start.13
  16.5 1.1 %collective-permute-done.4.refs_7_ = bf16[13,16,128]{2,1,0:T(8,128)(2,1)S(1)} collective-permute-done((bf16[13,16,128]{2,1,0:T(8,128)(2,1)S(1)}, bf16[13,16,128]{2,1,0:T(8,128)(2,1)S(1)}, u32[]{:S(2)}, u32[]{:S(2)}) %collective-permute-start.4) | collective-permute-done | bytes 53280 | tf_op jit(solution)/shard_map/ppermute | solution.py:128
  17.7 0.0 collective-permute-start.12
  17.7 0.8 %collective-permute-done.6.refs_9_ = bf16[13,16,128]{2,1,0:T(8,128)(2,1)S(1)} collective-permute-done((bf16[13,16,128]{2,1,0:T(8,128)(2,1)S(1)}, bf16[13,16,128]{2,1,0:T(8,128)(2,1)S(1)}, u32[]{:S(2)}, u32[]{:S(2)}) %collective-permute-start.6) | collective-permute-done | bytes 53280 | tf_op jit(solution)/shard_map/ppermute | solution.py:128
  18.4 0.0 collective-permute-start.14
  19.7 0.0 collective-permute-done.8.refs_11_
  19.7 0.0 collective-permute-done.13.refs_16_
  19.8 0.0 collective-permute-done.12.refs_15_
  19.8 0.0 collective-permute-done.10.refs_13_
  19.8 0.0 collective-permute-done.14.refs_17_
  19.8 0.0 copy-start
  19.8 0.8 %copy-done = bf16[13,16,128]{2,1,0:T(8,128)(2,1)S(1)} copy-done((bf16[13,16,128]{2,1,0:T(8,128)(2,1)S(1)}, bf16[13,16,128]{2,1,0:T(8,128)(2,1)}, u32[]{:S(2)}) %copy-start) | copy-done | bytes 53272
  20.6 1.8 %shard_map.77 = (f32[16,768]{1,0:T(8,128)}, f32[16,768]{1,0:T(8,128)}, f32[3]{0:T(128)}) custom-call(f32[1]{0:T(128)S(6)} %copy.8.refs_0_, f32[1]{0:T(128)S(6)} %copy.9.refs_1_, bf16[13,16,128]{2,1,0:T(8,128)(2,1)S(1)} %copy-done, bf16[13,16,128]{2,1,0:T(8,128)(2,1)S(1)} %collective-permute-done.refs_3_, ...), custom_call_target="tpu_custom_call" | custom-call | tf_op jit(solution)/shard_map/pallas_call | solution.py:142
Async XLA Ops:
  2.0 7.1 %collective-permute-start = (bf16[13,16,128]{2,1,0:T(8,128)(2,1)}, bf16[13,16,128]{2,1,0:T(8,128)(2,1)S(1)}, u32[]{:S(2)}, u32[]{:S(2)}) collective-permute-start(bf16[13,16,128]{2,1,0:T(8,128)(2,1)} %shard_map.76.refs_2_), channel_id=1, source_target_pairs={{0,8},{1,9},{2,10},{3,11},{4,12},{5,13},{6,14},{7,15},{8,0},{9,1},... | collective-permute-start | bytes 159752 | tf_op jit(solution)/shard_map/ppermute | solution.py:128
  6.1 4.6 %collective-permute-start.3 = (bf16[13,16,128]{2,1,0:T(8,128)(2,1)}, bf16[13,16,128]{2,1,0:T(8,128)(2,1)S(1)}, u32[]{:S(2)}, u32[]{:S(2)}) collective-permute-start(bf16[13,16,128]{2,1,0:T(8,128)(2,1)} %shard_map.76.refs_2_), channel_id=1, source_target_pairs={{0,2},{1,3},{2,0},{3,1},{4,6},{5,7},{6,4},{7,5},{8,10},{9,11},{10,... | collective-permute-start | bytes 159752 | tf_op jit(solution)/shard_map/ppermute | solution.py:128
  7.6 4.3 %collective-permute-start.1 = (bf16[13,16,128]{2,1,0:T(8,128)(2,1)}, bf16[13,16,128]{2,1,0:T(8,128)(2,1)S(1)}, u32[]{:S(2)}, u32[]{:S(2)}) collective-permute-start(bf16[13,16,128]{2,1,0:T(8,128)(2,1)} %shard_map.76.refs_2_), channel_id=1, source_target_pairs={{0,4},{1,5},{2,6},{3,7},{4,0},{5,1},{6,2},{7,3},{8,12},{9,13},{10,... | collective-permute-start | bytes 159752 | tf_op jit(solution)/shard_map/ppermute | solution.py:128
  9.1 3.3 %collective-permute-start.7 = (bf16[13,16,128]{2,1,0:T(8,128)(2,1)}, bf16[13,16,128]{2,1,0:T(8,128)(2,1)S(1)}, u32[]{:S(2)}, u32[]{:S(2)}) collective-permute-start(bf16[13,16,128]{2,1,0:T(8,128)(2,1)} %shard_map.76.refs_2_), channel_id=1, source_target_pairs={{0,1},{1,0},{2,3},{3,2},{4,5},{5,4},{6,7},{7,6},{8,9},{9,8},{10,11... | collective-permute-start | bytes 159752 | tf_op jit(solution)/shard_map/ppermute | solution.py:128
  9.1 4.8 %collective-permute-start.2 = (bf16[13,16,128]{2,1,0:T(8,128)(2,1)S(1)}, bf16[13,16,128]{2,1,0:T(8,128)(2,1)S(1)}, u32[]{:S(2)}, u32[]{:S(2)}) collective-permute-start(bf16[13,16,128]{2,1,0:T(8,128)(2,1)S(1)} %collective-permute-done.refs_3_), channel_id=1, source_target_pairs={{0,4},{1,5},{2,6},{3,7},{4,0},{5,1},{6,2},{7,3},{8,12},{9,13},{10,... | collective-permute-start | bytes 159752 | tf_op jit(solution)/shard_map/ppermute | solution.py:128
  10.6 4.2 %collective-permute-start.11 = (bf16[13,16,128]{2,1,0:T(8,128)(2,1)S(1)}, bf16[13,16,128]{2,1,0:T(8,128)(2,1)S(1)}, u32[]{:S(2)}, u32[]{:S(2)}) collective-permute-start(bf16[13,16,128]{2,1,0:T(8,128)(2,1)S(1)} %collective-permute-done.3.refs_6_), channel_id=1, source_target_pairs={{0,1},{1,0},{2,3},{3,2},{4,5},{5,4},{6,7},{7,6},{8,9},{9,8},{10,11... | collective-permute-start | bytes 159752 | tf_op jit(solution)/shard_map/ppermute | solution.py:128
  11.9 3.0 %collective-permute-start.9 = (bf16[13,16,128]{2,1,0:T(8,128)(2,1)S(1)}, bf16[13,16,128]{2,1,0:T(8,128)(2,1)S(1)}, u32[]{:S(2)}, u32[]{:S(2)}) collective-permute-start(bf16[13,16,128]{2,1,0:T(8,128)(2,1)S(1)} %collective-permute-done.1.refs_4_), channel_id=1, source_target_pairs={{0,1},{1,0},{2,3},{3,2},{4,5},{5,4},{6,7},{7,6},{8,9},{9,8},{10,11... | collective-permute-start | bytes 159752 | tf_op jit(solution)/shard_map/ppermute | solution.py:128
  11.9 4.6 %collective-permute-start.5 = (bf16[13,16,128]{2,1,0:T(8,128)(2,1)S(1)}, bf16[13,16,128]{2,1,0:T(8,128)(2,1)S(1)}, u32[]{:S(2)}, u32[]{:S(2)}) collective-permute-start(bf16[13,16,128]{2,1,0:T(8,128)(2,1)S(1)} %collective-permute-done.1.refs_4_), channel_id=1, source_target_pairs={{0,2},{1,3},{2,0},{3,1},{4,6},{5,7},{6,4},{7,5},{8,10},{9,11},{10,... | collective-permute-start | bytes 159752 | tf_op jit(solution)/shard_map/ppermute | solution.py:128
  12.4 5.2 %collective-permute-start.4 = (bf16[13,16,128]{2,1,0:T(8,128)(2,1)S(1)}, bf16[13,16,128]{2,1,0:T(8,128)(2,1)S(1)}, u32[]{:S(2)}, u32[]{:S(2)}) collective-permute-start(bf16[13,16,128]{2,1,0:T(8,128)(2,1)S(1)} %collective-permute-done.refs_3_), channel_id=1, source_target_pairs={{0,2},{1,3},{2,0},{3,1},{4,6},{5,7},{6,4},{7,5},{8,10},{9,11},{10,... | collective-permute-start | bytes 159752 | tf_op jit(solution)/shard_map/ppermute | solution.py:128
  13.9 4.5 %collective-permute-start.6 = (bf16[13,16,128]{2,1,0:T(8,128)(2,1)S(1)}, bf16[13,16,128]{2,1,0:T(8,128)(2,1)S(1)}, u32[]{:S(2)}, u32[]{:S(2)}) collective-permute-start(bf16[13,16,128]{2,1,0:T(8,128)(2,1)S(1)} %collective-permute-done.2.refs_5_), channel_id=1, source_target_pairs={{0,2},{1,3},{2,0},{3,1},{4,6},{5,7},{6,4},{7,5},{8,10},{9,11},{10,... | collective-permute-start | bytes 159752 | tf_op jit(solution)/shard_map/ppermute | solution.py:128
  14.9 4.9 %collective-permute-start.8 = (bf16[13,16,128]{2,1,0:T(8,128)(2,1)S(1)}, bf16[13,16,128]{2,1,0:T(8,128)(2,1)S(1)}, u32[]{:S(2)}, u32[]{:S(2)}) collective-permute-start(bf16[13,16,128]{2,1,0:T(8,128)(2,1)S(1)} %collective-permute-done.refs_3_), channel_id=1, source_target_pairs={{0,1},{1,0},{2,3},{3,2},{4,5},{5,4},{6,7},{7,6},{8,9},{9,8},{10,11... | collective-permute-start | bytes 159752 | tf_op jit(solution)/shard_map/ppermute | solution.py:128
  14.9 4.9 %collective-permute-start.10 = (bf16[13,16,128]{2,1,0:T(8,128)(2,1)S(1)}, bf16[13,16,128]{2,1,0:T(8,128)(2,1)S(1)}, u32[]{:S(2)}, u32[]{:S(2)}) collective-permute-start(bf16[13,16,128]{2,1,0:T(8,128)(2,1)S(1)} %collective-permute-done.2.refs_5_), channel_id=1, source_target_pairs={{0,1},{1,0},{2,3},{3,2},{4,5},{5,4},{6,7},{7,6},{8,9},{9,8},{10,11... | collective-permute-start | bytes 159752 | tf_op jit(solution)/shard_map/ppermute | solution.py:128
  16.5 3.2 %collective-permute-start.13 = (bf16[13,16,128]{2,1,0:T(8,128)(2,1)S(1)}, bf16[13,16,128]{2,1,0:T(8,128)(2,1)S(1)}, u32[]{:S(2)}, u32[]{:S(2)}) collective-permute-start(bf16[13,16,128]{2,1,0:T(8,128)(2,1)S(1)} %collective-permute-done.5.refs_8_), channel_id=1, source_target_pairs={{0,1},{1,0},{2,3},{3,2},{4,5},{5,4},{6,7},{7,6},{8,9},{9,8},{10,11... | collective-permute-start | bytes 159752 | tf_op jit(solution)/shard_map/ppermute | solution.py:128
  17.7 2.1 %collective-permute-start.12 = (bf16[13,16,128]{2,1,0:T(8,128)(2,1)S(1)}, bf16[13,16,128]{2,1,0:T(8,128)(2,1)S(1)}, u32[]{:S(2)}, u32[]{:S(2)}) collective-permute-start(bf16[13,16,128]{2,1,0:T(8,128)(2,1)S(1)} %collective-permute-done.4.refs_7_), channel_id=1, source_target_pairs={{0,1},{1,0},{2,3},{3,2},{4,5},{5,4},{6,7},{7,6},{8,9},{9,8},{10,11... | collective-permute-start | bytes 159752 | tf_op jit(solution)/shard_map/ppermute | solution.py:128
  18.4 1.3 %collective-permute-start.14 = (bf16[13,16,128]{2,1,0:T(8,128)(2,1)S(1)}, bf16[13,16,128]{2,1,0:T(8,128)(2,1)S(1)}, u32[]{:S(2)}, u32[]{:S(2)}) collective-permute-start(bf16[13,16,128]{2,1,0:T(8,128)(2,1)S(1)} %collective-permute-done.6.refs_9_), channel_id=1, source_target_pairs={{0,1},{1,0},{2,3},{3,2},{4,5},{5,4},{6,7},{7,6},{8,9},{9,8},{10,11... | collective-permute-start | bytes 159752 | tf_op jit(solution)/shard_map/ppermute | solution.py:128
  19.8 0.8 %copy-start = (bf16[13,16,128]{2,1,0:T(8,128)(2,1)S(1)}, bf16[13,16,128]{2,1,0:T(8,128)(2,1)}, u32[]{:S(2)}) copy-start(bf16[13,16,128]{2,1,0:T(8,128)(2,1)} %shard_map.76.refs_2_) | copy-start | bytes 159748

commit v2 on v1

--- a/solution.py
+++ b/solution.py
@@ -9,6 +9,11 @@
 LANES = 128
 VMEM = pl.BlockSpec(memory_space=pltpu.VMEM)
 SMEM = pl.BlockSpec(memory_space=pltpu.SMEM)
+HBM = pl.BlockSpec(memory_space=pltpu.HBM)
+
+
+def in_hbm(x):
+    return pltpu.with_memory_space_constraint(x, pltpu.HBM)
 
 
 def normalize(rows):
@@ -29,31 +34,44 @@
     return loss, jnp.where(matched, -sigma, sigma)
 
 
-def pack_kernel(mates_ref, img_ref, txt_ref, out_ref):
-    rows, width = img_ref.shape
+def pack_kernel(mates_hbm, img_hbm, txt_hbm, out_ref, mates_ref, mates_sem, sems):
+    rows, width = img_hbm.shape
     tiles = width // LANES
-    for t in range(tiles):
-        out_ref[t] = img_ref[:, t * LANES : (t + 1) * LANES]
-        out_ref[tiles + t] = txt_ref[:, t * LANES : (t + 1) * LANES]
+    copies = []
+    for i, source in enumerate((img_hbm, txt_hbm)):
+        for t in range(tiles):
+            at = i * tiles + t
+            copies.append(
+                pltpu.make_async_copy(
+                    source.at[:, t * LANES : (t + 1) * LANES], out_ref.at[at], sems.at[at]
+                )
+            )
+    indices = pltpu.make_async_copy(mates_hbm, mates_ref, mates_sem)
+    indices.start()
+    for copy in copies:
+        copy.start()
+    indices.wait()
     row = lax.broadcasted_iota(jnp.int32, (rows, LANES), 0)
     mates = jnp.zeros((rows, LANES), jnp.int32)
     for r in range(rows):
         mates = jnp.where(row == r, mates_ref[r], mates)
     out_ref[2 * tiles] = mates.astype(jnp.float32).astype(jnp.bfloat16)
-
-
-def pair_kernel(distances, narrow, sharp_ref, shift_ref, *refs):
-    blocks = refs[: len(distances)]
-    image_out, text_out, summary_out, img_half, txt_half, mates, weights = refs[len(distances) :]
-    count = len(distances)
+    for copy in copies:
+        copy.wait()
+
+
+def pair_kernel(held, narrow, scalars_ref, *refs):
+    count = sum(len(distances) for distances in held)
+    stacks, refs = refs[: len(held)], refs[len(held) :]
+    image_out, text_out, summary_out = refs[:3]
+    img_half, txt_half, mates, weights = refs[3:]
     rows, width = image_out.shape
     tiles = width // LANES
     total = rows * count
     me = lax.axis_index("wide") * narrow + lax.axis_index("narrow")
-    sharp, shift = sharp_ref[0], shift_ref[0]
-
-    def unit_tiles(block, first):
-        values = [block[first + t].astype(jnp.float32) for t in range(tiles)]
+
+    def unit_tiles(tile, first):
+        values = [tile(first + t).astype(jnp.float32) for t in range(tiles)]
         squares = values[0] * values[0]
         for v in values[1:]:
             squares = squares + v * v
@@ -61,20 +79,23 @@
         return [v * scales for v in values], scales
 
     own = None
-    for distance, block in zip(distances, blocks):
-        here = pl.ds(pl.multiple_of((me ^ distance) * rows, rows), rows)
-        img_units, img_scale = unit_tiles(block, 0)
-        txt_units, txt_scale = unit_tiles(block, tiles)
-        for t in range(tiles):
-            lanes = slice(t * LANES, (t + 1) * LANES)
-            img_half[here, lanes] = img_units[t].astype(jnp.bfloat16)
-            txt_half[here, lanes] = txt_units[t].astype(jnp.bfloat16)
-        mates[here, :] = block[2 * tiles].astype(jnp.float32)
-        if distance == 0:
-            own = (img_units, img_scale, txt_units, txt_scale)
+    for distances, stack in zip(held, stacks):
+        for place, distance in enumerate(distances):
+            tile = lambda t: stack[place * (2 * tiles + 1) + t]
+            here = pl.ds(pl.multiple_of((me ^ distance) * rows, rows), rows)
+            img_units, img_scale = unit_tiles(tile, 0)
+            txt_units, txt_scale = unit_tiles(tile, tiles)
+            for t in range(tiles):
+                lanes = slice(t * LANES, (t + 1) * LANES)
+                img_half[here, lanes] = img_units[t].astype(jnp.bfloat16)
+                txt_half[here, lanes] = txt_units[t].astype(jnp.bfloat16)
+            mates[here, :] = tile(2 * tiles).astype(jnp.float32)
+            if distance == 0:
+                own = (img_units, img_scale, txt_units, txt_scale)
 
     nt = (((1,), (1,)), ((), ()))
     cosine = lax.dot_general(img_half[...], txt_half[...], nt, preferred_element_type=jnp.float32)
+    sharp, shift = scalars_ref[0:1, :], scalars_ref[1:2, :]
     logit = sharp * cosine + shift
     column = lax.broadcasted_iota(jnp.int32, (total, LANES), 1).astype(jnp.float32)
     matched = jnp.concatenate(
@@ -119,26 +140,38 @@
     tiles = 2 * (width // LANES) + 1
     packed = pl.pallas_call(
         pack_kernel,
-        out_shape=jax.ShapeDtypeStruct((tiles, rows, LANES), jnp.bfloat16),
-        in_specs=[SMEM, VMEM, VMEM],
+        out_shape=pltpu.VMEM((tiles, rows, LANES), jnp.bfloat16),
+        in_specs=[HBM, HBM, HBM],
         out_specs=VMEM,
-    )(mates, images, texts)
+        scratch_shapes=[
+            pltpu.SMEM((rows,), jnp.int32),
+            pltpu.SemaphoreType.DMA,
+            pltpu.SemaphoreType.DMA((tiles - 1,)),
+        ],
+    )(*(in_hbm(x) for x in (mates, images, texts)))
 
     def swap(x, distance):
         return lax.ppermute(x, GROUP, [(i, i ^ distance) for i in range(count)])
 
-    held = {0: packed}
-    bit = narrow
-    held[2 * bit] = swap(packed, 2 * bit)
-    held[bit] = swap(packed, bit)
-    held[3 * bit] = swap(held[2 * bit], bit)
-    for bit in (2, 1):
-        for distance in list(held):
-            held[distance + bit] = swap(held[distance], bit)
-
-    distances = tuple(held)
     total = rows * count
-    kernel = lambda *refs: pair_kernel(distances, narrow, *refs)
+    scalars = jnp.stack([jnp.broadcast_to(v, (total,)) for v in (sharpness, offset)])
+    def join(*parts):
+        return tuple(d for ds, _ in parts for d in ds), jnp.concatenate([p for _, p in parts])
+
+    def send(part, distance):
+        return tuple(d ^ distance for d in part[0]), swap(part[1], distance)
+
+    z, x, c = narrow, 2, 1
+    own = ((0,), packed)
+    z3 = send(own, 3 * z)
+    z2 = send(own, 2 * z)
+    z1 = send(own, 1 * z)
+    early, late = join(own,z2), join(z1,z3)
+    xearly, xlate = send(early, x), send(late, x)
+    held = [early, late, xearly, xlate]
+    held += [send(h, c) for h in held]
+
+    kernel = lambda *refs: pair_kernel([d for d, _ in held], narrow, *refs)
     return pl.pallas_call(
         kernel,
         out_shape=(
@@ -146,7 +179,7 @@
             jax.ShapeDtypeStruct((rows, width), jnp.float32),
             jax.ShapeDtypeStruct((3,), jnp.float32),
         ),
-        in_specs=[SMEM, SMEM] + [VMEM] * count,
+        in_specs=[VMEM] * (1 + len(held)),
         out_specs=(VMEM, VMEM, SMEM),
         scratch_shapes=[
             pltpu.VMEM((total, width), jnp.bfloat16),
@@ -155,7 +188,7 @@
             pltpu.VMEM((total, total), jnp.bfloat16),
         ],
         compiler_params=pltpu.CompilerParams(vmem_limit_bytes=32 * 1024 * 1024),
-    )(sharpness, offset, *held.values())
+    )(scalars, *[x for _, x in held])
 
 
 def any_group(wide, narrow, images, texts, mates, sharpness, offset):

time: 22.7 us -> 20.1 us (0.89)
  starting transfers between devices: 12 us -> 9.53 us
  waiting for transfers between devices: 4.36 us -> 5.39 us
  local copies, waits for them, and re-layouts: 0.8 us -> 0.09 us
  Pallas kernels: 3.24 us -> 2.79 us
    ppermute x15 -> x9, starting transfers between devices: 12 us -> 9.53 us  [swap(): return lax.ppermute(x, GROUP, [(i, i ^ distance) for i in range(count)])]
    ppermute x15 -> x9, waiting for transfers between devices: 4.36 us -> 5.39 us  [swap(): return lax.ppermute(x, GROUP, [(i, i ^ distance) for i in range(count)])]
    unnamed x2 -> x1, local copies, waits for them, and re-layouts: 0.8 us -> 0.01 us
    pallas_call x1, Pallas kernels: 1.4 us -> 0.96 us  [small_group(): pl.pallas_call(pack_kernel, out_shape=pltpu.VMEM((tiles, rows, LANES), jn...]
  transfers between devices with their start and end apart: 15 -> 9, of which waited for: 4 -> 3; matrix products, arithmetic and copies ran while one was open for 0% -> 0% of each run, Pallas kernels for 0% -> 0%
where the time goes in v2:
time: 20.1 us; the launch traced here: 19.8 us
  starting transfers between devices  9.53 us (47%)
  waiting for transfers between devices  5.39 us (27%)
  Pallas kernels  2.79 us (14%)
  between operations  2 us (10%)
    ppermute x9, starting transfers between devices, swap(): return lax.ppermute(x, GROUP, [(i, i ^ distance) for i in range(count)])  9.53 us
    ppermute x9, waiting for transfers between devices, swap(): return lax.ppermute(x, GROUP, [(i, i ^ distance) for i in range(count)])  5.39 us
    pallas_call x1, Pallas kernels, small_group(): pl.pallas_call(kernel, out_shape=(jax.ShapeDtypeStruct((rows, width), jnp...  1.83 us
    pallas_call x1, Pallas kernels, small_group(): pl.pallas_call(pack_kernel, out_shape=pltpu.VMEM((tiles, rows, LANES), jn...  0.96 us
  transfers between devices with their start and end apart: 9, of which 3 were waited for; matrix products, arithmetic and copies ran while one was open for 0% of the time, Pallas kernels for 0%

profile of v2, /device:TPU:0, one launch (start us, length us, event | category | flops | bytes accessed | tf_op | source)
XLA Modules:
  0.0 19.8 jit_solution(12130575710105555766)
XLA Ops:
  0.6 1.0 %shard_map.79 = bf16[13,16,128]{2,1,0:T(8,128)(2,1)S(1)} custom-call(s32[16]{0:T(128)} %mates_hbm.1, bf16[16,768]{1,0:T(8,128)(2,1)} %img_hbm.1, bf16[16,768]{1,0:T(8,128)(2,1)} %txt_hbm.1), custom_call_target="tpu_custom_call" | custom-call | tf_op jit(solution)/shard_map/pallas_call | solution.py:141
  1.6 4.1 %collective-permute-start = (bf16[13,16,128]{2,1,0:T(8,128)(2,1)S(1)}, bf16[13,16,128]{2,1,0:T(8,128)(2,1)S(1)}, u32[]{:S(2)}, u32[]{:S(2)}) collective-permute-start(bf16[13,16,128]{2,1,0:T(8,128)(2,1)S(1)} %shard_map.79), channel_id=1, source_target_pairs={{0,8},{1,9},{2,10},{3,11},{4,12},{5,13},{6,14},{7,15},{8,0},{9,1},... | collective-permute-start | bytes 159752 | tf_op jit(solution)/shard_map/ppermute | solution.py:154
  5.7 1.3 %collective-permute-start.2 = (bf16[13,16,128]{2,1,0:T(8,128)(2,1)S(1)}, bf16[13,16,128]{2,1,0:T(8,128)(2,1)S(1)}, u32[]{:S(2)}, u32[]{:S(2)}) collective-permute-start(bf16[13,16,128]{2,1,0:T(8,128)(2,1)S(1)} %shard_map.79), channel_id=1, source_target_pairs={{0,12},{1,13},{2,14},{3,15},{4,8},{5,9},{6,10},{7,11},{8,4},{9,5},... | collective-permute-start | bytes 159752 | tf_op jit(solution)/shard_map/ppermute | solution.py:154
  7.0 0.2 %collective-permute-start.1 = (bf16[13,16,128]{2,1,0:T(8,128)(2,1)S(1)}, bf16[13,16,128]{2,1,0:T(8,128)(2,1)S(1)}, u32[]{:S(2)}, u32[]{:S(2)}) collective-permute-start(bf16[13,16,128]{2,1,0:T(8,128)(2,1)S(1)} %shard_map.79), channel_id=1, source_target_pairs={{0,4},{1,5},{2,6},{3,7},{4,0},{5,1},{6,2},{7,3},{8,12},{9,13},{10,... | collective-permute-start | bytes 159752 | tf_op jit(solution)/shard_map/ppermute | solution.py:154
  7.3 1.1 %collective-permute-done = bf16[13,16,128]{2,1,0:T(8,128)(2,1)S(1)} collective-permute-done((bf16[13,16,128]{2,1,0:T(8,128)(2,1)S(1)}, bf16[13,16,128]{2,1,0:T(8,128)(2,1)S(1)}, u32[]{:S(2)}, u32[]{:S(2)}) %collective-permute-start) | collective-permute-done | bytes 53280 | tf_op jit(solution)/shard_map/ppermute | solution.py:154
  8.4 1.8 %collective-permute-start.3 = (bf16[26,16,128]{2,1,0:T(8,128)(2,1)S(1)}, bf16[26,16,128]{2,1,0:T(8,128)(2,1)S(1)}, u32[]{:S(2)}, u32[]{:S(2)}) collective-permute-start(bf16[26,16,128]{2,1,0:T(8,128)(2,1)S(1)} %pad_maximum_fusion.refs_1_), channel_id=1, source_target_pairs={{0,2},{1,3},{2,0},{3,1},{4,6},{5,7},{6,4},{7,5},{8,10},{9,11},{10,... | collective-permute-start | bytes 319496 | tf_op jit(solution)/shard_map/ppermute | solution.py:154
  10.2 1.6 %collective-permute-done.1 = bf16[13,16,128]{2,1,0:T(8,128)(2,1)S(1)} collective-permute-done((bf16[13,16,128]{2,1,0:T(8,128)(2,1)S(1)}, bf16[13,16,128]{2,1,0:T(8,128)(2,1)S(1)}, u32[]{:S(2)}, u32[]{:S(2)}) %collective-permute-start.1) | collective-permute-done | bytes 53280 | tf_op jit(solution)/shard_map/ppermute | solution.py:154
  11.8 0.0 collective-permute-done.2
  11.8 1.6 %collective-permute-start.4 = (bf16[26,16,128]{2,1,0:T(8,128)(2,1)S(1)}, bf16[26,16,128]{2,1,0:T(8,128)(2,1)S(1)}, u32[]{:S(2)}, u32[]{:S(2)}) collective-permute-start(bf16[26,16,128]{2,1,0:T(8,128)(2,1)S(1)} %constant_dynamic-update-slice_fusion.refs_2_), channel_id=1, source_target_pairs={{0,2},{1,3},{2,0},{3,1},{4,6},{5,7},{6,4},{7,5},{8,10},{9,11},{10,... | collective-permute-start | bytes 319496 | tf_op jit(solution)/shard_map/ppermute | solution.py:154
  13.3 0.0 collective-permute-start.5
  13.3 0.5 %collective-permute-start.6 = (bf16[26,16,128]{2,1,0:T(8,128)(2,1)S(1)}, bf16[26,16,128]{2,1,0:T(8,128)(2,1)S(1)}, u32[]{:S(2)}, u32[]{:S(2)}) collective-permute-start(bf16[26,16,128]{2,1,0:T(8,128)(2,1)S(1)} %constant_dynamic-update-slice_fusion.refs_2_), channel_id=1, source_target_pairs={{0,1},{1,0},{2,3},{3,2},{4,5},{5,4},{6,7},{7,6},{8,9},{9,8},{10,11... | collective-permute-start | bytes 319496 | tf_op jit(solution)/shard_map/ppermute | solution.py:154
  13.8 0.0 collective-permute-done.3.refs_3_
  13.9 0.0 collective-permute-start.7
  13.9 2.7 %collective-permute-done.4.refs_4_ = bf16[26,16,128]{2,1,0:T(8,128)(2,1)S(1)} collective-permute-done((bf16[26,16,128]{2,1,0:T(8,128)(2,1)S(1)}, bf16[26,16,128]{2,1,0:T(8,128)(2,1)S(1)}, u32[]{:S(2)}, u32[]{:S(2)}) %collective-permute-start.4) | collective-permute-done | bytes 106528 | tf_op jit(solution)/shard_map/ppermute | solution.py:154
  16.6 0.0 collective-permute-start.8
  17.9 0.0 collective-permute-done.5.refs_5_
  17.9 0.0 collective-permute-done.6.refs_6_
  17.9 0.0 collective-permute-done.7.refs_7_
  17.9 0.0 collective-permute-done.8.refs_8_
  17.9 0.1 stack.6.refs_0_
  18.0 1.8 %shard_map.80 = (f32[16,768]{1,0:T(8,128)}, f32[16,768]{1,0:T(8,128)}, f32[3]{0:T(128)}) custom-call(f32[2,256]{1,0:T(2,128)S(1)} %stack.6.refs_0_, bf16[26,16,128]{2,1,0:T(8,128)(2,1)S(1)} %pad_maximum_fusion.refs_1_, bf16[26,16,128]{2,1,0:T(8,128)(2,1)S(1)} %constant_dynamic-update-slice_fusion.refs_2_, ...), custom_call_target="tpu_custom_call" | custom-call | tf_op jit(solution)/shard_map/pallas_call | solution.py:175
  (4 shorter events, 0.0 us)
Async XLA Ops:
  1.6 6.8 %collective-permute-start = (bf16[13,16,128]{2,1,0:T(8,128)(2,1)S(1)}, bf16[13,16,128]{2,1,0:T(8,128)(2,1)S(1)}, u32[]{:S(2)}, u32[]{:S(2)}) collective-permute-start(bf16[13,16,128]{2,1,0:T(8,128)(2,1)S(1)} %shard_map.79), channel_id=1, source_target_pairs={{0,8},{1,9},{2,10},{3,11},{4,12},{5,13},{6,14},{7,15},{8,0},{9,1},... | collective-permute-start | bytes 159752 | tf_op jit(solution)/shard_map/ppermute | solution.py:154
  5.7 6.1 %collective-permute-start.2 = (bf16[13,16,128]{2,1,0:T(8,128)(2,1)S(1)}, bf16[13,16,128]{2,1,0:T(8,128)(2,1)S(1)}, u32[]{:S(2)}, u32[]{:S(2)}) collective-permute-start(bf16[13,16,128]{2,1,0:T(8,128)(2,1)S(1)} %shard_map.79), channel_id=1, source_target_pairs={{0,12},{1,13},{2,14},{3,15},{4,8},{5,9},{6,10},{7,11},{8,4},{9,5},... | collective-permute-start | bytes 159752 | tf_op jit(solution)/shard_map/ppermute | solution.py:154
  7.0 4.7 %collective-permute-start.1 = (bf16[13,16,128]{2,1,0:T(8,128)(2,1)S(1)}, bf16[13,16,128]{2,1,0:T(8,128)(2,1)S(1)}, u32[]{:S(2)}, u32[]{:S(2)}) collective-permute-start(bf16[13,16,128]{2,1,0:T(8,128)(2,1)S(1)} %shard_map.79), channel_id=1, source_target_pairs={{0,4},{1,5},{2,6},{3,7},{4,0},{5,1},{6,2},{7,3},{8,12},{9,13},{10,... | collective-permute-start | bytes 159752 | tf_op jit(solution)/shard_map/ppermute | solution.py:154
  8.4 5.5 %collective-permute-start.3 = (bf16[26,16,128]{2,1,0:T(8,128)(2,1)S(1)}, bf16[26,16,128]{2,1,0:T(8,128)(2,1)S(1)}, u32[]{:S(2)}, u32[]{:S(2)}) collective-permute-start(bf16[26,16,128]{2,1,0:T(8,128)(2,1)S(1)} %pad_maximum_fusion.refs_1_), channel_id=1, source_target_pairs={{0,2},{1,3},{2,0},{3,1},{4,6},{5,7},{6,4},{7,5},{8,10},{9,11},{10,... | collective-permute-start | bytes 319496 | tf_op jit(solution)/shard_map/ppermute | solution.py:154
  11.8 4.8 %collective-permute-start.4 = (bf16[26,16,128]{2,1,0:T(8,128)(2,1)S(1)}, bf16[26,16,128]{2,1,0:T(8,128)(2,1)S(1)}, u32[]{:S(2)}, u32[]{:S(2)}) collective-permute-start(bf16[26,16,128]{2,1,0:T(8,128)(2,1)S(1)} %constant_dynamic-update-slice_fusion.refs_2_), channel_id=1, source_target_pairs={{0,2},{1,3},{2,0},{3,1},{4,6},{5,7},{6,4},{7,5},{8,10},{9,11},{10,... | collective-permute-start | bytes 319496 | tf_op jit(solution)/shard_map/ppermute | solution.py:154
  13.3 4.5 %collective-permute-start.5 = (bf16[26,16,128]{2,1,0:T(8,128)(2,1)S(1)}, bf16[26,16,128]{2,1,0:T(8,128)(2,1)S(1)}, u32[]{:S(2)}, u32[]{:S(2)}) collective-permute-start(bf16[26,16,128]{2,1,0:T(8,128)(2,1)S(1)} %pad_maximum_fusion.refs_1_), channel_id=1, source_target_pairs={{0,1},{1,0},{2,3},{3,2},{4,5},{5,4},{6,7},{7,6},{8,9},{9,8},{10,11... | collective-permute-start | bytes 319496 | tf_op jit(solution)/shard_map/ppermute | solution.py:154
  13.3 4.5 %collective-permute-start.6 = (bf16[26,16,128]{2,1,0:T(8,128)(2,1)S(1)}, bf16[26,16,128]{2,1,0:T(8,128)(2,1)S(1)}, u32[]{:S(2)}, u32[]{:S(2)}) collective-permute-start(bf16[26,16,128]{2,1,0:T(8,128)(2,1)S(1)} %constant_dynamic-update-slice_fusion.refs_2_), channel_id=1, source_target_pairs={{0,1},{1,0},{2,3},{3,2},{4,5},{5,4},{6,7},{7,6},{8,9},{9,8},{10,11... | collective-permute-start | bytes 319496 | tf_op jit(solution)/shard_map/ppermute | solution.py:154
  13.9 4.0 %collective-permute-start.7 = (bf16[26,16,128]{2,1,0:T(8,128)(2,1)S(1)}, bf16[26,16,128]{2,1,0:T(8,128)(2,1)S(1)}, u32[]{:S(2)}, u32[]{:S(2)}) collective-permute-start(bf16[26,16,128]{2,1,0:T(8,128)(2,1)S(1)} %collective-permute-done.3.refs_3_), channel_id=1, source_target_pairs={{0,1},{1,0},{2,3},{3,2},{4,5},{5,4},{6,7},{7,6},{8,9},{9,8},{10,11... | collective-permute-start | bytes 319496 | tf_op jit(solution)/shard_map/ppermute | solution.py:154
  16.6 1.3 %collective-permute-start.8 = (bf16[26,16,128]{2,1,0:T(8,128)(2,1)S(1)}, bf16[26,16,128]{2,1,0:T(8,128)(2,1)S(1)}, u32[]{:S(2)}, u32[]{:S(2)}) collective-permute-start(bf16[26,16,128]{2,1,0:T(8,128)(2,1)S(1)} %collective-permute-done.4.refs_4_), channel_id=1, source_target_pairs={{0,1},{1,0},{2,3},{3,2},{4,5},{5,4},{6,7},{7,6},{8,9},{9,8},{10,11... | collective-permute-start | bytes 319496 | tf_op jit(solution)/shard_map/ppermute | solution.py:154

commit v3 on v2

--- a/solution.py
+++ b/solution.py
@@ -12,6 +12,10 @@
 HBM = pl.BlockSpec(memory_space=pltpu.HBM)
 
 
+def in_vmem(x):
+    return pltpu.with_memory_space_constraint(x, pltpu.VMEM)
+
+
 def in_hbm(x):
     return pltpu.with_memory_space_constraint(x, pltpu.HBM)
 
@@ -36,16 +40,10 @@
 
 def pack_kernel(mates_hbm, img_hbm, txt_hbm, out_ref, mates_ref, mates_sem, sems):
     rows, width = img_hbm.shape
-    tiles = width // LANES
-    copies = []
-    for i, source in enumerate((img_hbm, txt_hbm)):
-        for t in range(tiles):
-            at = i * tiles + t
-            copies.append(
-                pltpu.make_async_copy(
-                    source.at[:, t * LANES : (t + 1) * LANES], out_ref.at[at], sems.at[at]
-                )
-            )
+    copies = [
+        pltpu.make_async_copy(source, out_ref.at[:, i * width : (i + 1) * width], sems.at[i])
+        for i, source in enumerate((img_hbm, txt_hbm))
+    ]
     indices = pltpu.make_async_copy(mates_hbm, mates_ref, mates_sem)
     indices.start()
     for copy in copies:
@@ -55,14 +53,14 @@
     mates = jnp.zeros((rows, LANES), jnp.int32)
     for r in range(rows):
         mates = jnp.where(row == r, mates_ref[r], mates)
-    out_ref[2 * tiles] = mates.astype(jnp.float32).astype(jnp.bfloat16)
+    out_ref[:, 2 * width :] = mates.astype(jnp.float32).astype(jnp.bfloat16)
     for copy in copies:
         copy.wait()
 
 
-def pair_kernel(held, narrow, scalars_ref, *refs):
+def pair_kernel(held, extra, narrow, scalars_ref, *refs):
     count = sum(len(distances) for distances in held)
-    stacks, refs = refs[: len(held)], refs[len(held) :]
+    stacks, refs = refs[: len(held)], refs[len(held) + extra :]
     image_out, text_out, summary_out = refs[:3]
     img_half, txt_half, mates, weights = refs[3:]
     rows, width = image_out.shape
@@ -81,7 +79,7 @@
     own = None
     for distances, stack in zip(held, stacks):
         for place, distance in enumerate(distances):
-            tile = lambda t: stack[place * (2 * tiles + 1) + t]
+            tile = lambda t: stack[place * rows : (place + 1) * rows, t * LANES : (t + 1) * LANES]
             here = pl.ds(pl.multiple_of((me ^ distance) * rows, rows), rows)
             img_units, img_scale = unit_tiles(tile, 0)
             txt_units, txt_scale = unit_tiles(tile, tiles)
@@ -102,10 +100,10 @@
         [mates[...] == column + float(c * LANES) for c in range(total // LANES)], axis=1
     )
     loss, slope = pair_terms(cosine, logit, matched)
+    weights[...] = (sharp * slope).astype(jnp.bfloat16)
     summary_out[0] = jnp.sum(loss) / total
     summary_out[1] = jnp.sum(slope * cosine)
     summary_out[2] = jnp.sum(slope)
-    weights[...] = (sharp * slope).astype(jnp.bfloat16)
 
     mine = pl.ds(pl.multiple_of(me * rows, rows), rows)
     picked = (
@@ -137,16 +135,15 @@
 def small_group(wide, narrow, images, texts, mates, sharpness, offset):
     rows, width = images.shape
     count = wide * narrow
-    tiles = 2 * (width // LANES) + 1
     packed = pl.pallas_call(
         pack_kernel,
-        out_shape=pltpu.VMEM((tiles, rows, LANES), jnp.bfloat16),
+        out_shape=pltpu.VMEM((rows, 2 * width + LANES), jnp.bfloat16),
         in_specs=[HBM, HBM, HBM],
         out_specs=VMEM,
         scratch_shapes=[
             pltpu.SMEM((rows,), jnp.int32),
             pltpu.SemaphoreType.DMA,
-            pltpu.SemaphoreType.DMA((tiles - 1,)),
+            pltpu.SemaphoreType.DMA((2,)),
         ],
     )(*(in_hbm(x) for x in (mates, images, texts)))
 
@@ -155,6 +152,7 @@
 
     total = rows * count
     scalars = jnp.stack([jnp.broadcast_to(v, (total,)) for v in (sharpness, offset)])
+    extras = ()
     def join(*parts):
         return tuple(d for ds, _ in parts for d in ds), jnp.concatenate([p for _, p in parts])
 
@@ -166,12 +164,14 @@
     z3 = send(own, 3 * z)
     z2 = send(own, 2 * z)
     z1 = send(own, 1 * z)
-    early, late = join(own,z2), join(z1,z3)
+    early, late = join(own,z3), join(z1,z2)
+    part, scalars = lax.optimization_barrier((early[1], scalars))
+    early = (early[0], part)
     xearly, xlate = send(early, x), send(late, x)
     held = [early, late, xearly, xlate]
     held += [send(h, c) for h in held]
 
-    kernel = lambda *refs: pair_kernel([d for d, _ in held], narrow, *refs)
+    kernel = lambda *refs: pair_kernel([d for d, _ in held], len(extras), narrow, *refs)
     return pl.pallas_call(
         kernel,
         out_shape=(
@@ -179,7 +179,7 @@
             jax.ShapeDtypeStruct((rows, width), jnp.float32),
             jax.ShapeDtypeStruct((3,), jnp.float32),
         ),
-        in_specs=[VMEM] * (1 + len(held)),
+        in_specs=[VMEM] * (1 + len(held) + len(extras)),
         out_specs=(VMEM, VMEM, SMEM),
         scratch_shapes=[
             pltpu.VMEM((total, width), jnp.bfloat16),
@@ -188,7 +188,7 @@
             pltpu.VMEM((total, total), jnp.bfloat16),
         ],
         compiler_params=pltpu.CompilerParams(vmem_limit_bytes=32 * 1024 * 1024),
-    )(scalars, *[x for _, x in held])
+    )(scalars, *[x for _, x in held], *extras)
 
 
 def any_group(wide, narrow, images, texts, mates, sharpness, offset):

time: 20.1 us -> 19.7 us (0.980)
  waiting for transfers between devices: 5.39 us -> 5.11 us
    ppermute x9, waiting for transfers between devices: 5.39 us -> 5.11 us  [swap(): return lax.ppermute(x, GROUP, [(i, i ^ distance) for i in range(count)])]
  transfers between devices with their start and end apart: 9 -> 9, of which waited for: 3 -> 5; matrix products, arithmetic and copies ran while one was open for 0% -> 1% of each run, Pallas kernels for 0% -> 0%
where the time goes in v3:
time: 19.7 us; the launch traced here: 19.5 us
  starting transfers between devices  9.63 us (49%)
  waiting for transfers between devices  5.11 us (26%)
  Pallas kernels  2.7 us (14%)
  between operations  1.97 us (10%)
    ppermute x9, starting transfers between devices, swap(): return lax.ppermute(x, GROUP, [(i, i ^ distance) for i in range(count)])  9.63 us
    ppermute x9, waiting for transfers between devices, swap(): return lax.ppermute(x, GROUP, [(i, i ^ distance) for i in range(count)])  5.11 us
    pallas_call x1, Pallas kernels, small_group(): pl.pallas_call(kernel, out_shape=(jax.ShapeDtypeStruct((rows, width), jnp...  1.86 us
    pallas_call x1, Pallas kernels, small_group(): pl.pallas_call(pack_kernel, out_shape=pltpu.VMEM((rows, 2 * width + LANES...  0.84 us
  transfers between devices with their start and end apart: 9, of which 5 were waited for; matrix products, arithmetic and copies ran while one was open for 1% of the time, Pallas kernels for 0%

profile of v3, /device:TPU:0, one launch (start us, length us, event | category | flops | bytes accessed | tf_op | source)
XLA Modules:
  0.0 19.5 jit_solution(15902167580709899271)
XLA Ops:
  0.6 0.8 %shard_map.79 = bf16[16,1664]{1,0:T(8,128)(2,1)S(1)} custom-call(s32[16]{0:T(128)} %mates_hbm.1, bf16[16,768]{1,0:T(8,128)(2,1)} %img_hbm.1, bf16[16,768]{1,0:T(8,128)(2,1)} %txt_hbm.1), custom_call_target="tpu_custom_call" | custom-call | tf_op jit(solution)/shard_map/pallas_call | solution.py:138
  1.5 5.1 %collective-permute-start = (bf16[16,1664]{1,0:T(8,128)(2,1)S(1)}, bf16[16,1664]{1,0:T(8,128)(2,1)S(1)}, u32[]{:S(2)}, u32[]{:S(2)}) collective-permute-start(bf16[16,1664]{1,0:T(8,128)(2,1)S(1)} %shard_map.79), channel_id=1, source_target_pairs={{0,12},{1,13},{2,14},{3,15},{4,8},{5,9},{6,10},{7,11},{8,4},{9,5},... | collective-permute-start | bytes 159752 | tf_op jit(solution)/shard_map/ppermute | solution.py:151
  6.6 0.0 collective-permute-start.2
  6.6 0.6 %collective-permute-start.1 = (bf16[16,1664]{1,0:T(8,128)(2,1)S(1)}, bf16[16,1664]{1,0:T(8,128)(2,1)S(1)}, u32[]{:S(2)}, u32[]{:S(2)}) collective-permute-start(bf16[16,1664]{1,0:T(8,128)(2,1)S(1)} %shard_map.79), channel_id=1, source_target_pairs={{0,4},{1,5},{2,6},{3,7},{4,0},{5,1},{6,2},{7,3},{8,12},{9,13},{10,... | collective-permute-start | bytes 159752 | tf_op jit(solution)/shard_map/ppermute | solution.py:151
  8.5 0.4 %collective-permute-done = bf16[16,1664]{1,0:T(8,128)(2,1)S(1)} collective-permute-done((bf16[16,1664]{1,0:T(8,128)(2,1)S(1)}, bf16[16,1664]{1,0:T(8,128)(2,1)S(1)}, u32[]{:S(2)}, u32[]{:S(2)}) %collective-permute-start) | collective-permute-done | bytes 53280 | tf_op jit(solution)/shard_map/ppermute | solution.py:151
  8.9 0.1 stack.6.refs_0_
  9.0 1.9 %collective-permute-start.3 = (bf16[32,1664]{1,0:T(8,128)(2,1)S(1)}, bf16[32,1664]{1,0:T(8,128)(2,1)S(1)}, u32[]{:S(2)}, u32[]{:S(2)}) collective-permute-start(bf16[32,1664]{1,0:T(8,128)(2,1)S(1)} %pad_maximum_fusion.refs_1_), channel_id=1, source_target_pairs={{0,2},{1,3},{2,0},{3,1},{4,6},{5,7},{6,4},{7,5},{8,10},{9,11},{10,... | collective-permute-start | bytes 319496 | tf_op jit(solution)/shard_map/ppermute | solution.py:151
  10.9 0.0 collective-permute-done.1
  10.9 0.8 %collective-permute-done.2 = bf16[16,1664]{1,0:T(8,128)(2,1)S(1)} collective-permute-done((bf16[16,1664]{1,0:T(8,128)(2,1)S(1)}, bf16[16,1664]{1,0:T(8,128)(2,1)S(1)}, u32[]{:S(2)}, u32[]{:S(2)}) %collective-permute-start.2) | collective-permute-done | bytes 53280 | tf_op jit(solution)/shard_map/ppermute | solution.py:151
  11.6 1.5 %collective-permute-start.4 = (bf16[32,1664]{1,0:T(8,128)(2,1)S(1)}, bf16[32,1664]{1,0:T(8,128)(2,1)S(1)}, u32[]{:S(2)}, u32[]{:S(2)}) collective-permute-start(bf16[32,1664]{1,0:T(8,128)(2,1)S(1)} %constant_dynamic-update-slice_fusion.refs_2_), channel_id=1, source_target_pairs={{0,2},{1,3},{2,0},{3,1},{4,6},{5,7},{6,4},{7,5},{8,10},{9,11},{10,... | collective-permute-start | bytes 319496 | tf_op jit(solution)/shard_map/ppermute | solution.py:151
  13.1 0.0 collective-permute-start.5
  13.1 0.5 %collective-permute-start.6 = (bf16[32,1664]{1,0:T(8,128)(2,1)S(1)}, bf16[32,1664]{1,0:T(8,128)(2,1)S(1)}, u32[]{:S(2)}, u32[]{:S(2)}) collective-permute-start(bf16[32,1664]{1,0:T(8,128)(2,1)S(1)} %constant_dynamic-update-slice_fusion.refs_2_), channel_id=1, source_target_pairs={{0,1},{1,0},{2,3},{3,2},{4,5},{5,4},{6,7},{7,6},{8,9},{9,8},{10,11... | collective-permute-start | bytes 319496 | tf_op jit(solution)/shard_map/ppermute | solution.py:151
  13.6 0.6 %collective-permute-done.3.refs_3_ = bf16[32,1664]{1,0:T(8,128)(2,1)S(1)} collective-permute-done((bf16[32,1664]{1,0:T(8,128)(2,1)S(1)}, bf16[32,1664]{1,0:T(8,128)(2,1)S(1)}, u32[]{:S(2)}, u32[]{:S(2)}) %collective-permute-start.3) | collective-permute-done | bytes 106528 | tf_op jit(solution)/shard_map/ppermute | solution.py:151
  14.2 0.0 collective-permute-start.7
  14.2 2.1 %collective-permute-done.4.refs_4_ = bf16[32,1664]{1,0:T(8,128)(2,1)S(1)} collective-permute-done((bf16[32,1664]{1,0:T(8,128)(2,1)S(1)}, bf16[32,1664]{1,0:T(8,128)(2,1)S(1)}, u32[]{:S(2)}, u32[]{:S(2)}) %collective-permute-start.4) | collective-permute-done | bytes 106528 | tf_op jit(solution)/shard_map/ppermute | solution.py:151
  16.3 0.0 collective-permute-start.8
  16.3 0.0 collective-permute-done.5.refs_5_
  16.3 0.0 collective-permute-done.6.refs_6_
  16.4 0.0 collective-permute-done.7.refs_7_
  16.4 1.3 %collective-permute-done.8.refs_8_ = bf16[32,1664]{1,0:T(8,128)(2,1)S(1)} collective-permute-done((bf16[32,1664]{1,0:T(8,128)(2,1)S(1)}, bf16[32,1664]{1,0:T(8,128)(2,1)S(1)}, u32[]{:S(2)}, u32[]{:S(2)}) %collective-permute-start.8) | collective-permute-done | bytes 106528 | tf_op jit(solution)/shard_map/ppermute | solution.py:151
  17.7 1.9 %shard_map.80 = (f32[16,768]{1,0:T(8,128)}, f32[16,768]{1,0:T(8,128)}, f32[3]{0:T(128)}) custom-call(f32[2,256]{1,0:T(2,128)S(1)} %stack.6.refs_0_, bf16[32,1664]{1,0:T(8,128)(2,1)S(1)} %pad_maximum_fusion.refs_1_, bf16[32,1664]{1,0:T(8,128)(2,1)S(1)} %constant_dynamic-update-slice_fusion.refs_2_, bf16[32,1664]{1,0:T(8,128)(2,1)S(1)} %collective-permute-done.3.refs_3_, ...), custom_call_target="tpu_custom_call" | custom-call | tf_op jit(solution)/shard_map/pallas_call | solution.py:175
  (4 shorter events, 0.0 us)
Async XLA Ops:
  1.5 7.4 %collective-permute-start = (bf16[16,1664]{1,0:T(8,128)(2,1)S(1)}, bf16[16,1664]{1,0:T(8,128)(2,1)S(1)}, u32[]{:S(2)}, u32[]{:S(2)}) collective-permute-start(bf16[16,1664]{1,0:T(8,128)(2,1)S(1)} %shard_map.79), channel_id=1, source_target_pairs={{0,12},{1,13},{2,14},{3,15},{4,8},{5,9},{6,10},{7,11},{8,4},{9,5},... | collective-permute-start | bytes 159752 | tf_op jit(solution)/shard_map/ppermute | solution.py:151
  6.6 5.0 %collective-permute-start.2 = (bf16[16,1664]{1,0:T(8,128)(2,1)S(1)}, bf16[16,1664]{1,0:T(8,128)(2,1)S(1)}, u32[]{:S(2)}, u32[]{:S(2)}) collective-permute-start(bf16[16,1664]{1,0:T(8,128)(2,1)S(1)} %shard_map.79), channel_id=1, source_target_pairs={{0,8},{1,9},{2,10},{3,11},{4,12},{5,13},{6,14},{7,15},{8,0},{9,1},... | collective-permute-start | bytes 159752 | tf_op jit(solution)/shard_map/ppermute | solution.py:151
  6.6 4.3 %collective-permute-start.1 = (bf16[16,1664]{1,0:T(8,128)(2,1)S(1)}, bf16[16,1664]{1,0:T(8,128)(2,1)S(1)}, u32[]{:S(2)}, u32[]{:S(2)}) collective-permute-start(bf16[16,1664]{1,0:T(8,128)(2,1)S(1)} %shard_map.79), channel_id=1, source_target_pairs={{0,4},{1,5},{2,6},{3,7},{4,0},{5,1},{6,2},{7,3},{8,12},{9,13},{10,... | collective-permute-start | bytes 159752 | tf_op jit(solution)/shard_map/ppermute | solution.py:151
  9.0 5.2 %collective-permute-start.3 = (bf16[32,1664]{1,0:T(8,128)(2,1)S(1)}, bf16[32,1664]{1,0:T(8,128)(2,1)S(1)}, u32[]{:S(2)}, u32[]{:S(2)}) collective-permute-start(bf16[32,1664]{1,0:T(8,128)(2,1)S(1)} %pad_maximum_fusion.refs_1_), channel_id=1, source_target_pairs={{0,2},{1,3},{2,0},{3,1},{4,6},{5,7},{6,4},{7,5},{8,10},{9,11},{10,... | collective-permute-start | bytes 319496 | tf_op jit(solution)/shard_map/ppermute | solution.py:151
  11.6 4.7 %collective-permute-start.4 = (bf16[32,1664]{1,0:T(8,128)(2,1)S(1)}, bf16[32,1664]{1,0:T(8,128)(2,1)S(1)}, u32[]{:S(2)}, u32[]{:S(2)}) collective-permute-start(bf16[32,1664]{1,0:T(8,128)(2,1)S(1)} %constant_dynamic-update-slice_fusion.refs_2_), channel_id=1, source_target_pairs={{0,2},{1,3},{2,0},{3,1},{4,6},{5,7},{6,4},{7,5},{8,10},{9,11},{10,... | collective-permute-start | bytes 319496 | tf_op jit(solution)/shard_map/ppermute | solution.py:151
  13.1 3.2 %collective-permute-start.5 = (bf16[32,1664]{1,0:T(8,128)(2,1)S(1)}, bf16[32,1664]{1,0:T(8,128)(2,1)S(1)}, u32[]{:S(2)}, u32[]{:S(2)}) collective-permute-start(bf16[32,1664]{1,0:T(8,128)(2,1)S(1)} %pad_maximum_fusion.refs_1_), channel_id=1, source_target_pairs={{0,1},{1,0},{2,3},{3,2},{4,5},{5,4},{6,7},{7,6},{8,9},{9,8},{10,11... | collective-permute-start | bytes 319496 | tf_op jit(solution)/shard_map/ppermute | solution.py:151
  13.1 3.2 %collective-permute-start.6 = (bf16[32,1664]{1,0:T(8,128)(2,1)S(1)}, bf16[32,1664]{1,0:T(8,128)(2,1)S(1)}, u32[]{:S(2)}, u32[]{:S(2)}) collective-permute-start(bf16[32,1664]{1,0:T(8,128)(2,1)S(1)} %constant_dynamic-update-slice_fusion.refs_2_), channel_id=1, source_target_pairs={{0,1},{1,0},{2,3},{3,2},{4,5},{5,4},{6,7},{7,6},{8,9},{9,8},{10,11... | collective-permute-start | bytes 319496 | tf_op jit(solution)/shard_map/ppermute | solution.py:151
  14.2 2.1 %collective-permute-start.7 = (bf16[32,1664]{1,0:T(8,128)(2,1)S(1)}, bf16[32,1664]{1,0:T(8,128)(2,1)S(1)}, u32[]{:S(2)}, u32[]{:S(2)}) collective-permute-start(bf16[32,1664]{1,0:T(8,128)(2,1)S(1)} %collective-permute-done.3.refs_3_), channel_id=1, source_target_pairs={{0,1},{1,0},{2,3},{3,2},{4,5},{5,4},{6,7},{7,6},{8,9},{9,8},{10,11... | collective-permute-start | bytes 319496 | tf_op jit(solution)/shard_map/ppermute | solution.py:151
  16.3 1.3 %collective-permute-start.8 = (bf16[32,1664]{1,0:T(8,128)(2,1)S(1)}, bf16[32,1664]{1,0:T(8,128)(2,1)S(1)}, u32[]{:S(2)}, u32[]{:S(2)}) collective-permute-start(bf16[32,1664]{1,0:T(8,128)(2,1)S(1)} %collective-permute-done.4.refs_4_), channel_id=1, source_target_pairs={{0,1},{1,0},{2,3},{3,2},{4,5},{5,4},{6,7},{7,6},{8,9},{9,8},{10,11... | collective-permute-start | bytes 319496 | tf_op jit(solution)/shard_map/ppermute | solution.py:151

commit v4 on v3

--- a/solution.py
+++ b/solution.py
@@ -10,10 +10,6 @@
 VMEM = pl.BlockSpec(memory_space=pltpu.VMEM)
 SMEM = pl.BlockSpec(memory_space=pltpu.SMEM)
 HBM = pl.BlockSpec(memory_space=pltpu.HBM)
-
-
-def in_vmem(x):
-    return pltpu.with_memory_space_constraint(x, pltpu.VMEM)
 
 
 def in_hbm(x):
@@ -58,9 +54,9 @@
         copy.wait()
 
 
-def pair_kernel(held, extra, narrow, scalars_ref, *refs):
-    count = sum(len(distances) for distances in held)
-    stacks, refs = refs[: len(held)], refs[len(held) + extra :]
+def pair_kernel(held, narrow, scalars_ref, *refs):
+    count = sum(len(origins) for origins in held)
+    stacks, refs = refs[: len(held)], refs[len(held) :]
     image_out, text_out, summary_out = refs[:3]
     img_half, txt_half, mates, weights = refs[3:]
     rows, width = image_out.shape
@@ -77,10 +73,14 @@
         return [v * scales for v in values], scales
 
     own = None
-    for distances, stack in zip(held, stacks):
-        for place, distance in enumerate(distances):
+    for origins, stack in zip(held, stacks):
+        for place, (sources, flip) in enumerate(origins):
             tile = lambda t: stack[place * rows : (place + 1) * rows, t * LANES : (t + 1) * LANES]
-            here = pl.ds(pl.multiple_of((me ^ distance) * rows, rows), rows)
+            origin = jnp.int32(sources[0])
+            for z, source in enumerate(sources[1:], 1):
+                origin = jnp.where(me // narrow == z, source, origin)
+            slot = origin * narrow + ((me % narrow) ^ flip)
+            here = pl.ds(pl.multiple_of(slot * rows, rows), rows)
             img_units, img_scale = unit_tiles(tile, 0)
             txt_units, txt_scale = unit_tiles(tile, tiles)
             for t in range(tiles):
@@ -88,7 +88,7 @@
                 img_half[here, lanes] = img_units[t].astype(jnp.bfloat16)
                 txt_half[here, lanes] = txt_units[t].astype(jnp.bfloat16)
             mates[here, :] = tile(2 * tiles).astype(jnp.float32)
-            if distance == 0:
+            if own is None:
                 own = (img_units, img_scale, txt_units, txt_scale)
 
     nt = (((1,), (1,)), ((), ()))
@@ -106,16 +106,21 @@
     summary_out[2] = jnp.sum(slope)
 
     mine = pl.ds(pl.multiple_of(me * rows, rows), rows)
-    picked = (
-        lax.broadcasted_iota(jnp.int32, (rows, total), 1)
-        == lax.broadcasted_iota(jnp.int32, (rows, total), 0) + me * rows
-    )
-    text_weights = lax.dot_general(
-        picked.astype(jnp.float32).astype(jnp.bfloat16),
-        weights[...],
+    first_lane = (lax.broadcasted_iota(jnp.int32, (rows, LANES), 1) == 0).astype(jnp.float32)
+    partner = lax.dot_general(
+        first_lane.astype(jnp.bfloat16),
+        mates[...].astype(jnp.bfloat16),
         nt,
         preferred_element_type=jnp.float32,
-    ).astype(jnp.bfloat16)
+    )
+    own_text = lax.broadcasted_iota(jnp.int32, (rows, total), 0) + me * rows
+    turned = lax.dot_general(
+        txt_half[mine, :], img_half[...], nt, preferred_element_type=jnp.float32
+    )
+    turned_slope = pair_terms(
+        turned, sharp * turned + shift, partner == own_text.astype(jnp.float32)
+    )[1]
+    text_weights = (sharp * turned_slope).astype(jnp.bfloat16)
     img_grad = jnp.dot(weights[mine, :], txt_half[...], preferred_element_type=jnp.float32)
     txt_grad = jnp.dot(text_weights, img_half[...], preferred_element_type=jnp.float32)
 
@@ -152,26 +157,30 @@
 
     total = rows * count
     scalars = jnp.stack([jnp.broadcast_to(v, (total,)) for v in (sharpness, offset)])
-    extras = ()
+
     def join(*parts):
         return tuple(d for ds, _ in parts for d in ds), jnp.concatenate([p for _, p in parts])
 
-    def send(part, distance):
-        return tuple(d ^ distance for d in part[0]), swap(part[1], distance)
-
-    z, x, c = narrow, 2, 1
-    own = ((0,), packed)
-    z3 = send(own, 3 * z)
-    z2 = send(own, 2 * z)
-    z1 = send(own, 1 * z)
-    early, late = join(own,z3), join(z1,z2)
-    part, scalars = lax.optimization_barrier((early[1], scalars))
-    early = (early[0], part)
-    xearly, xlate = send(early, x), send(late, x)
+    def turned(part, sources):
+        pairs = [(sources[z] * narrow + n, z * narrow + n) for z in range(wide) for n in range(narrow)]
+        return tuple((sources, f) for _, f in part[0]), lax.ppermute(part[1], GROUP, pairs)
+
+    def send(part, flip):
+        return tuple((s, f ^ flip) for s, f in part[0]), swap(part[1], flip)
+
+    chip, core = 2, 1
+    own = (((tuple(range(wide)), 0),), packed)
+    first = turned(own, (3, 2, 0, 1))
+    third = turned(own, (2, 3, 1, 0))
+    near = turned(own, (1, 0, 3, 2))
+    early, late = join(own, first), join(near, third)
+    blocks, scalars = lax.optimization_barrier((early[1], scalars))
+    early = (early[0], blocks)
+    xearly, xlate = send(early, chip), send(late, chip)
     held = [early, late, xearly, xlate]
-    held += [send(h, c) for h in held]
-
-    kernel = lambda *refs: pair_kernel([d for d, _ in held], len(extras), narrow, *refs)
+    held += [send(h, core) for h in held]
+
+    kernel = lambda *refs: pair_kernel([d for d, _ in held], narrow, *refs)
     return pl.pallas_call(
         kernel,
         out_shape=(
@@ -179,7 +188,7 @@
             jax.ShapeDtypeStruct((rows, width), jnp.float32),
             jax.ShapeDtypeStruct((3,), jnp.float32),
         ),
-        in_specs=[VMEM] * (1 + len(held) + len(extras)),
+        in_specs=[VMEM] * (1 + len(held)),
         out_specs=(VMEM, VMEM, SMEM),
         scratch_shapes=[
             pltpu.VMEM((total, width), jnp.bfloat16),
@@ -188,7 +197,7 @@
             pltpu.VMEM((total, total), jnp.bfloat16),
         ],
         compiler_params=pltpu.CompilerParams(vmem_limit_bytes=32 * 1024 * 1024),
-    )(scalars, *[x for _, x in held], *extras)
+    )(scalars, *[part for _, part in held])
 
 
 def any_group(wide, narrow, images, texts, mates, sharpness, offset):

time: 19.7 us -> 19.4 us (0.985)
    ppermute x9 -> x6, starting transfers between devices: 9.63 us -> 3.86 us  [swap(): return lax.ppermute(x, GROUP, [(i, i ^ distance) for i in range(count)])]
    ppermute x0 -> x3, starting transfers between devices: none -> 5.67 us  [turned(): lax.ppermute(part[1], GROUP, pairs)]
    ppermute x9 -> x6, waiting for transfers between devices: 5.11 us -> 3.99 us  [swap(): return lax.ppermute(x, GROUP, [(i, i ^ distance) for i in range(count)])]
    ppermute x0 -> x3, waiting for transfers between devices: none -> 1.01 us  [turned(): lax.ppermute(part[1], GROUP, pairs)]
where the time goes in v4:
time: 19.4 us; the launch traced here: 19.2 us
  starting transfers between devices  9.53 us (49%)
  waiting for transfers between devices  5 us (26%)
  Pallas kernels  2.64 us (14%)
  between operations  1.97 us (10%)
    ppermute x3, starting transfers between devices, turned(): lax.ppermute(part[1], GROUP, pairs)  5.67 us
    ppermute x6, waiting for transfers between devices, swap(): return lax.ppermute(x, GROUP, [(i, i ^ distance) for i in range(count)])  3.99 us
    ppermute x6, starting transfers between devices, swap(): return lax.ppermute(x, GROUP, [(i, i ^ distance) for i in range(count)])  3.86 us
    pallas_call x1, Pallas kernels, small_group(): pl.pallas_call(kernel, out_shape=(jax.ShapeDtypeStruct((rows, width), jnp...  1.8 us
    ppermute x3, waiting for transfers between devices, turned(): lax.ppermute(part[1], GROUP, pairs)  1.01 us
    pallas_call x1, Pallas kernels, small_group(): pl.pallas_call(pack_kernel, out_shape=pltpu.VMEM((rows, 2 * width + LANES...  0.84 us
  transfers between devices with their start and end apart: 9, of which 5 were waited for; matrix products, arithmetic and copies ran while one was open for 1% of the time, Pallas kernels for 0%

profile of v4, /device:TPU:0, one launch (start us, length us, event | category | flops | bytes accessed | tf_op | source)
XLA Modules:
  0.0 19.2 jit_solution(17841424952521795982)
XLA Ops:
  0.6 0.8 %shard_map.79 = bf16[16,1664]{1,0:T(8,128)(2,1)S(1)} custom-call(s32[16]{0:T(128)} %mates_hbm.1, bf16[16,768]{1,0:T(8,128)(2,1)} %img_hbm.1, bf16[16,768]{1,0:T(8,128)(2,1)} %txt_hbm.1), custom_call_target="tpu_custom_call" | custom-call | tf_op jit(solution)/shard_map/pallas_call | solution.py:143
  1.5 4.1 %collective-permute-start = (bf16[16,1664]{1,0:T(8,128)(2,1)S(1)}, bf16[16,1664]{1,0:T(8,128)(2,1)S(1)}, u32[]{:S(2)}, u32[]{:S(2)}) collective-permute-start(bf16[16,1664]{1,0:T(8,128)(2,1)S(1)} %shard_map.79), channel_id=1, source_target_pairs={{12,0},{13,1},{14,2},{15,3},{8,4},{9,5},{10,6},{11,7},{0,8},{1,9},... | collective-permute-start | bytes 159752 | tf_op jit(solution)/shard_map/ppermute | solution.py:166
  5.6 1.1 %collective-permute-start.2 = (bf16[16,1664]{1,0:T(8,128)(2,1)S(1)}, bf16[16,1664]{1,0:T(8,128)(2,1)S(1)}, u32[]{:S(2)}, u32[]{:S(2)}) collective-permute-start(bf16[16,1664]{1,0:T(8,128)(2,1)S(1)} %shard_map.79), channel_id=1, source_target_pairs={{8,0},{9,1},{10,2},{11,3},{12,4},{13,5},{14,6},{15,7},{4,8},{5,9},... | collective-permute-start | bytes 159752 | tf_op jit(solution)/shard_map/ppermute | solution.py:166
  6.6 0.5 %collective-permute-start.1 = (bf16[16,1664]{1,0:T(8,128)(2,1)S(1)}, bf16[16,1664]{1,0:T(8,128)(2,1)S(1)}, u32[]{:S(2)}, u32[]{:S(2)}) collective-permute-start(bf16[16,1664]{1,0:T(8,128)(2,1)S(1)} %shard_map.79), channel_id=1, source_target_pairs={{4,0},{5,1},{6,2},{7,3},{0,4},{1,5},{2,6},{3,7},{12,8},{13,9},{14,... | collective-permute-start | bytes 159752 | tf_op jit(solution)/shard_map/ppermute | solution.py:166
  8.5 0.3 %collective-permute-done = bf16[16,1664]{1,0:T(8,128)(2,1)S(1)} collective-permute-done((bf16[16,1664]{1,0:T(8,128)(2,1)S(1)}, bf16[16,1664]{1,0:T(8,128)(2,1)S(1)}, u32[]{:S(2)}, u32[]{:S(2)}) %collective-permute-start) | collective-permute-done | bytes 53280 | tf_op jit(solution)/shard_map/ppermute | solution.py:166
  8.8 0.1 stack.6.refs_0_
  8.8 1.8 %collective-permute-start.3 = (bf16[32,1664]{1,0:T(8,128)(2,1)S(1)}, bf16[32,1664]{1,0:T(8,128)(2,1)S(1)}, u32[]{:S(2)}, u32[]{:S(2)}) collective-permute-start(bf16[32,1664]{1,0:T(8,128)(2,1)S(1)} %pad_maximum_fusion.refs_1_), channel_id=1, source_target_pairs={{0,2},{1,3},{2,0},{3,1},{4,6},{5,7},{6,4},{7,5},{8,10},{9,11},{10,... | collective-permute-start | bytes 319496 | tf_op jit(solution)/shard_map/ppermute | solution.py:156
  10.6 0.7 %collective-permute-done.1 = bf16[16,1664]{1,0:T(8,128)(2,1)S(1)} collective-permute-done((bf16[16,1664]{1,0:T(8,128)(2,1)S(1)}, bf16[16,1664]{1,0:T(8,128)(2,1)S(1)}, u32[]{:S(2)}, u32[]{:S(2)}) %collective-permute-start.1) | collective-permute-done | bytes 53280 | tf_op jit(solution)/shard_map/ppermute | solution.py:166
  11.3 0.0 collective-permute-done.2
  11.4 1.6 %collective-permute-start.4 = (bf16[32,1664]{1,0:T(8,128)(2,1)S(1)}, bf16[32,1664]{1,0:T(8,128)(2,1)S(1)}, u32[]{:S(2)}, u32[]{:S(2)}) collective-permute-start(bf16[32,1664]{1,0:T(8,128)(2,1)S(1)} %constant_dynamic-update-slice_fusion.refs_2_), channel_id=1, source_target_pairs={{0,2},{1,3},{2,0},{3,1},{4,6},{5,7},{6,4},{7,5},{8,10},{9,11},{10,... | collective-permute-start | bytes 319496 | tf_op jit(solution)/shard_map/ppermute | solution.py:156
  12.9 0.0 collective-permute-start.5
  12.9 0.5 %collective-permute-start.6 = (bf16[32,1664]{1,0:T(8,128)(2,1)S(1)}, bf16[32,1664]{1,0:T(8,128)(2,1)S(1)}, u32[]{:S(2)}, u32[]{:S(2)}) collective-permute-start(bf16[32,1664]{1,0:T(8,128)(2,1)S(1)} %constant_dynamic-update-slice_fusion.refs_2_), channel_id=1, source_target_pairs={{0,1},{1,0},{2,3},{3,2},{4,5},{5,4},{6,7},{7,6},{8,9},{9,8},{10,11... | collective-permute-start | bytes 319496 | tf_op jit(solution)/shard_map/ppermute | solution.py:156
  13.4 1.0 %collective-permute-done.3.refs_3_ = bf16[32,1664]{1,0:T(8,128)(2,1)S(1)} collective-permute-done((bf16[32,1664]{1,0:T(8,128)(2,1)S(1)}, bf16[32,1664]{1,0:T(8,128)(2,1)S(1)}, u32[]{:S(2)}, u32[]{:S(2)}) %collective-permute-start.3) | collective-permute-done | bytes 106528 | tf_op jit(solution)/shard_map/ppermute | solution.py:156
  14.4 0.0 collective-permute-start.7
  14.4 1.7 %collective-permute-done.4.refs_4_ = bf16[32,1664]{1,0:T(8,128)(2,1)S(1)} collective-permute-done((bf16[32,1664]{1,0:T(8,128)(2,1)S(1)}, bf16[32,1664]{1,0:T(8,128)(2,1)S(1)}, u32[]{:S(2)}, u32[]{:S(2)}) %collective-permute-start.4) | collective-permute-done | bytes 106528 | tf_op jit(solution)/shard_map/ppermute | solution.py:156
  16.1 0.0 collective-permute-start.8
  16.1 0.0 collective-permute-done.5.refs_5_
  16.1 0.0 collective-permute-done.6.refs_6_
  16.1 0.0 collective-permute-done.7.refs_7_
  16.2 1.3 %collective-permute-done.8.refs_8_ = bf16[32,1664]{1,0:T(8,128)(2,1)S(1)} collective-permute-done((bf16[32,1664]{1,0:T(8,128)(2,1)S(1)}, bf16[32,1664]{1,0:T(8,128)(2,1)S(1)}, u32[]{:S(2)}, u32[]{:S(2)}) %collective-permute-start.8) | collective-permute-done | bytes 106528 | tf_op jit(solution)/shard_map/ppermute | solution.py:156
  17.4 1.8 %shard_map.80 = (f32[16,768]{1,0:T(8,128)}, f32[16,768]{1,0:T(8,128)}, f32[3]{0:T(128)}) custom-call(f32[2,256]{1,0:T(2,128)S(1)} %stack.6.refs_0_, bf16[32,1664]{1,0:T(8,128)(2,1)S(1)} %pad_maximum_fusion.refs_1_, bf16[32,1664]{1,0:T(8,128)(2,1)S(1)} %constant_dynamic-update-slice_fusion.refs_2_, bf16[32,1664]{1,0:T(8,128)(2,1)S(1)} %collective-permute-done.3.refs_3_, ...), custom_call_target="tpu_custom_call" | custom-call | tf_op jit(solution)/shard_map/pallas_call | solution.py:184
  (4 shorter events, 0.0 us)
Async XLA Ops:
  1.5 7.3 %collective-permute-start = (bf16[16,1664]{1,0:T(8,128)(2,1)S(1)}, bf16[16,1664]{1,0:T(8,128)(2,1)S(1)}, u32[]{:S(2)}, u32[]{:S(2)}) collective-permute-start(bf16[16,1664]{1,0:T(8,128)(2,1)S(1)} %shard_map.79), channel_id=1, source_target_pairs={{12,0},{13,1},{14,2},{15,3},{8,4},{9,5},{10,6},{11,7},{0,8},{1,9},... | collective-permute-start | bytes 159752 | tf_op jit(solution)/shard_map/ppermute | solution.py:166
  5.6 5.8 %collective-permute-start.2 = (bf16[16,1664]{1,0:T(8,128)(2,1)S(1)}, bf16[16,1664]{1,0:T(8,128)(2,1)S(1)}, u32[]{:S(2)}, u32[]{:S(2)}) collective-permute-start(bf16[16,1664]{1,0:T(8,128)(2,1)S(1)} %shard_map.79), channel_id=1, source_target_pairs={{8,0},{9,1},{10,2},{11,3},{12,4},{13,5},{14,6},{15,7},{4,8},{5,9},... | collective-permute-start | bytes 159752 | tf_op jit(solution)/shard_map/ppermute | solution.py:166
  6.6 4.7 %collective-permute-start.1 = (bf16[16,1664]{1,0:T(8,128)(2,1)S(1)}, bf16[16,1664]{1,0:T(8,128)(2,1)S(1)}, u32[]{:S(2)}, u32[]{:S(2)}) collective-permute-start(bf16[16,1664]{1,0:T(8,128)(2,1)S(1)} %shard_map.79), channel_id=1, source_target_pairs={{4,0},{5,1},{6,2},{7,3},{0,4},{1,5},{2,6},{3,7},{12,8},{13,9},{14,... | collective-permute-start | bytes 159752 | tf_op jit(solution)/shard_map/ppermute | solution.py:166
  8.8 5.6 %collective-permute-start.3 = (bf16[32,1664]{1,0:T(8,128)(2,1)S(1)}, bf16[32,1664]{1,0:T(8,128)(2,1)S(1)}, u32[]{:S(2)}, u32[]{:S(2)}) collective-permute-start(bf16[32,1664]{1,0:T(8,128)(2,1)S(1)} %pad_maximum_fusion.refs_1_), channel_id=1, source_target_pairs={{0,2},{1,3},{2,0},{3,1},{4,6},{5,7},{6,4},{7,5},{8,10},{9,11},{10,... | collective-permute-start | bytes 319496 | tf_op jit(solution)/shard_map/ppermute | solution.py:156
  11.4 4.8 %collective-permute-start.4 = (bf16[32,1664]{1,0:T(8,128)(2,1)S(1)}, bf16[32,1664]{1,0:T(8,128)(2,1)S(1)}, u32[]{:S(2)}, u32[]{:S(2)}) collective-permute-start(bf16[32,1664]{1,0:T(8,128)(2,1)S(1)} %constant_dynamic-update-slice_fusion.refs_2_), channel_id=1, source_target_pairs={{0,2},{1,3},{2,0},{3,1},{4,6},{5,7},{6,4},{7,5},{8,10},{9,11},{10,... | collective-permute-start | bytes 319496 | tf_op jit(solution)/shard_map/ppermute | solution.py:156
  12.9 3.2 %collective-permute-start.5 = (bf16[32,1664]{1,0:T(8,128)(2,1)S(1)}, bf16[32,1664]{1,0:T(8,128)(2,1)S(1)}, u32[]{:S(2)}, u32[]{:S(2)}) collective-permute-start(bf16[32,1664]{1,0:T(8,128)(2,1)S(1)} %pad_maximum_fusion.refs_1_), channel_id=1, source_target_pairs={{0,1},{1,0},{2,3},{3,2},{4,5},{5,4},{6,7},{7,6},{8,9},{9,8},{10,11... | collective-permute-start | bytes 319496 | tf_op jit(solution)/shard_map/ppermute | solution.py:156
  12.9 3.2 %collective-permute-start.6 = (bf16[32,1664]{1,0:T(8,128)(2,1)S(1)}, bf16[32,1664]{1,0:T(8,128)(2,1)S(1)}, u32[]{:S(2)}, u32[]{:S(2)}) collective-permute-start(bf16[32,1664]{1,0:T(8,128)(2,1)S(1)} %constant_dynamic-update-slice_fusion.refs_2_), channel_id=1, source_target_pairs={{0,1},{1,0},{2,3},{3,2},{4,5},{5,4},{6,7},{7,6},{8,9},{9,8},{10,11... | collective-permute-start | bytes 319496 | tf_op jit(solution)/shard_map/ppermute | solution.py:156
  14.4 1.8 %collective-permute-start.7 = (bf16[32,1664]{1,0:T(8,128)(2,1)S(1)}, bf16[32,1664]{1,0:T(8,128)(2,1)S(1)}, u32[]{:S(2)}, u32[]{:S(2)}) collective-permute-start(bf16[32,1664]{1,0:T(8,128)(2,1)S(1)} %collective-permute-done.3.refs_3_), channel_id=1, source_target_pairs={{0,1},{1,0},{2,3},{3,2},{4,5},{5,4},{6,7},{7,6},{8,9},{9,8},{10,11... | collective-permute-start | bytes 319496 | tf_op jit(solution)/shard_map/ppermute | solution.py:156
  16.1 1.3 %collective-permute-start.8 = (bf16[32,1664]{1,0:T(8,128)(2,1)S(1)}, bf16[32,1664]{1,0:T(8,128)(2,1)S(1)}, u32[]{:S(2)}, u32[]{:S(2)}) collective-permute-start(bf16[32,1664]{1,0:T(8,128)(2,1)S(1)} %collective-permute-done.4.refs_4_), channel_id=1, source_target_pairs={{0,1},{1,0},{2,3},{3,2},{4,5},{5,4},{6,7},{7,6},{8,9},{9,8},{10,11... | collective-permute-start | bytes 319496 | tf_op jit(solution)/shard_map/ppermute | solution.py:156

commit v5 on v4

--- a/solution.py
+++ b/solution.py
@@ -10,6 +10,10 @@
 VMEM = pl.BlockSpec(memory_space=pltpu.VMEM)
 SMEM = pl.BlockSpec(memory_space=pltpu.SMEM)
 HBM = pl.BlockSpec(memory_space=pltpu.HBM)
+
+
+def in_vmem(x):
+    return pltpu.with_memory_space_constraint(x, pltpu.VMEM)
 
 
 def in_hbm(x):
@@ -54,16 +58,22 @@
         copy.wait()
 
 
-def pair_kernel(held, narrow, scalars_ref, *refs):
-    count = sum(len(origins) for origins in held)
-    stacks, refs = refs[: len(held)], refs[len(held) :]
-    image_out, text_out, summary_out = refs[:3]
-    img_half, txt_half, mates, weights = refs[3:]
-    rows, width = image_out.shape
-    tiles = width // LANES
-    total = rows * count
-    me = lax.axis_index("wide") * narrow + lax.axis_index("narrow")
-
+def unit_rows(block, tiles):
+    parts = []
+    for first in (0, tiles):
+        values = [
+            block[0 : block.shape[0] // 2, (first + t) * LANES : (first + t + 1) * LANES].astype(jnp.float32)
+            for t in range(tiles)
+        ]
+        squares = values[0] * values[0]
+        for v in values[1:]:
+            squares = squares + v * v
+        scales = lax.rsqrt(jnp.sum(squares, axis=1, keepdims=True) + 1e-06)
+        parts += [[v * scales for v in values], scales]
+    return parts
+
+
+def place_blocks(held, stacks, img_half, txt_half, mates, me, rows, tiles):
     def unit_tiles(tile, first):
         values = [tile(first + t).astype(jnp.float32) for t in range(tiles)]
         squares = values[0] * values[0]
@@ -72,15 +82,11 @@
         scales = lax.rsqrt(jnp.sum(squares, axis=1, keepdims=True) + 1e-06)
         return [v * scales for v in values], scales
 
-    own = None
+    first_block = None
     for origins, stack in zip(held, stacks):
-        for place, (sources, flip) in enumerate(origins):
+        for place, slot in enumerate(origins):
             tile = lambda t: stack[place * rows : (place + 1) * rows, t * LANES : (t + 1) * LANES]
-            origin = jnp.int32(sources[0])
-            for z, source in enumerate(sources[1:], 1):
-                origin = jnp.where(me // narrow == z, source, origin)
-            slot = origin * narrow + ((me % narrow) ^ flip)
-            here = pl.ds(pl.multiple_of(slot * rows, rows), rows)
+            here = pl.ds(pl.multiple_of(slot(me) * rows, rows), rows)
             img_units, img_scale = unit_tiles(tile, 0)
             txt_units, txt_scale = unit_tiles(tile, tiles)
             for t in range(tiles):
@@ -88,8 +94,26 @@
                 img_half[here, lanes] = img_units[t].astype(jnp.bfloat16)
                 txt_half[here, lanes] = txt_units[t].astype(jnp.bfloat16)
             mates[here, :] = tile(2 * tiles).astype(jnp.float32)
-            if own is None:
-                own = (img_units, img_scale, txt_units, txt_scale)
+            if first_block is None:
+                first_block = (img_units, img_scale, txt_units, txt_scale)
+    return first_block
+
+
+def early_kernel(held, narrow, rows, width, *refs):
+    me = lax.axis_index("wide") * narrow + lax.axis_index("narrow")
+    place_blocks(held, refs[: len(held)], *refs[len(held) :], me, rows, width // LANES)
+
+
+def pair_kernel(held, count, narrow, scalars_ref, own_ref, *refs):
+    stacks, refs = refs[: len(held)], refs[len(held) + 3 :]
+    image_out, text_out, summary_out, img_half, txt_half, mates, weights = refs
+    rows, width = image_out.shape
+    tiles = width // LANES
+    total = rows * count
+    me = lax.axis_index("wide") * narrow + lax.axis_index("narrow")
+
+    own = unit_rows(own_ref, tiles)
+    place_blocks(held, stacks, img_half, txt_half, mates, me, rows, tiles)
 
     nt = (((1,), (1,)), ((), ()))
     cosine = lax.dot_general(img_half[...], txt_half[...], nt, preferred_element_type=jnp.float32)
@@ -157,47 +181,71 @@
 
     total = rows * count
     scalars = jnp.stack([jnp.broadcast_to(v, (total,)) for v in (sharpness, offset)])
-
-    def join(*parts):
-        return tuple(d for ds, _ in parts for d in ds), jnp.concatenate([p for _, p in parts])
-
-    def turned(part, sources):
-        pairs = [(sources[z] * narrow + n, z * narrow + n) for z in range(wide) for n in range(narrow)]
-        return tuple((sources, f) for _, f in part[0]), lax.ppermute(part[1], GROUP, pairs)
-
-    def send(part, flip):
-        return tuple((s, f ^ flip) for s, f in part[0]), swap(part[1], flip)
-
     chip, core = 2, 1
-    own = (((tuple(range(wide)), 0),), packed)
-    first = turned(own, (3, 2, 0, 1))
-    third = turned(own, (2, 3, 1, 0))
-    near = turned(own, (1, 0, 3, 2))
-    early, late = join(own, first), join(near, third)
-    blocks, scalars = lax.optimization_barrier((early[1], scalars))
-    early = (early[0], blocks)
-    xearly, xlate = send(early, chip), send(late, chip)
-    held = [early, late, xearly, xlate]
-    held += [send(h, core) for h in held]
-
-    kernel = lambda *refs: pair_kernel([d for d, _ in held], narrow, *refs)
+    stay = tuple(range(wide))
+
+    def place(me, sources, flip):
+        origin = jnp.int32(sources[0])
+        for z, source in enumerate(sources[1:], 1):
+            origin = jnp.where(me // narrow == z, source, origin)
+        return origin * narrow + ((me % narrow) ^ flip)
+
+    def slot(even_from, odd_from):
+        return lambda me: jnp.where(me % 2 == 1, place(me, *odd_from), place(me, *even_from))
+
+    def move(blocks, even_from, odd_from):
+        pairs = []
+        for z in range(wide):
+            for n in range(narrow):
+                sources, flip = odd_from if n % 2 else even_from
+                pairs.append((sources[z] * narrow + (n ^ flip), z * narrow + n))
+        return lax.ppermute(blocks, GROUP, pairs)
+
+    def across(slots, blocks):
+        return [lambda me, f=f: f(me ^ core) for f in slots], swap(blocks, core)
+
+    even_from, odd_from = ((3, 2, 0, 1), (1, 0, 3, 2), (2, 3, 1, 0)), ((3, 2, 0, 1), (1, 0, 3, 2), (2, 3, 1, 0))
+    froms = [((e, 0), (o, 0)) for e, o in zip(even_from, odd_from)]
+    own_slot = slot((stay, 0), (stay, 0))
+    first = move(packed, *froms[0])
+    third = move(packed, *froms[2])
+    near = move(packed, *froms[1])
+    early, late = jnp.concatenate([packed, first]), jnp.concatenate([near, third])
+    early, scalars = lax.optimization_barrier((early, scalars))
+    pairs = [[own_slot, slot(*froms[0])], [slot(*froms[1]), slot(*froms[2])]]
+    flipped = [[lambda me, f=f: f(me ^ chip) for f in p] for p in pairs]
+    held = [(pairs[0], early), (pairs[1], late)]
+    held += [(flipped[0], swap(early, chip)), (flipped[1], swap(late, chip))]
+    held += [across(*part) for part in held]
+
+    early_count = len(held) - 1
+    halves = pl.pallas_call(
+        lambda *refs: early_kernel([d for d, _ in held[:-1]], narrow, rows, width, *refs),
+        out_shape=(
+            pltpu.VMEM((total, width), jnp.bfloat16),
+            pltpu.VMEM((total, width), jnp.bfloat16),
+            pltpu.VMEM((total, LANES), jnp.float32),
+        ),
+        in_specs=[VMEM] * early_count,
+        out_specs=(VMEM, VMEM, VMEM),
+    )(*[in_vmem(part) for _, part in held[:-1]])
+    last = held[-1:]
     return pl.pallas_call(
-        kernel,
+        lambda *refs: pair_kernel([d for d, _ in last], count, narrow, *refs),
         out_shape=(
             jax.ShapeDtypeStruct((rows, width), jnp.float32),
             jax.ShapeDtypeStruct((rows, width), jnp.float32),
             jax.ShapeDtypeStruct((3,), jnp.float32),
+            pltpu.VMEM((total, width), jnp.bfloat16),
+            pltpu.VMEM((total, width), jnp.bfloat16),
+            pltpu.VMEM((total, LANES), jnp.float32),
         ),
-        in_specs=[VMEM] * (1 + len(held)),
-        out_specs=(VMEM, VMEM, SMEM),
-        scratch_shapes=[
-            pltpu.VMEM((total, width), jnp.bfloat16),
-            pltpu.VMEM((total, width), jnp.bfloat16),
-            pltpu.VMEM((total, LANES), jnp.float32),
-            pltpu.VMEM((total, total), jnp.bfloat16),
-        ],
+        in_specs=[VMEM] * 6,
+        out_specs=(VMEM, VMEM, SMEM, VMEM, VMEM, VMEM),
+        input_output_aliases={3: 3, 4: 4, 5: 5},
+        scratch_shapes=[pltpu.VMEM((total, total), jnp.bfloat16)],
         compiler_params=pltpu.CompilerParams(vmem_limit_bytes=32 * 1024 * 1024),
-    )(scalars, *[part for _, part in held])
+    )(scalars, in_vmem(held[0][1]), last[0][1], *[in_vmem(h) for h in halves])[:3]
 
 
 def any_group(wide, narrow, images, texts, mates, sharpness, offset):

time: 19.4 us -> 19.3 us (level)
  waiting for transfers between devices: 5 us -> 4.74 us
    ppermute x6, waiting for transfers between devices: 3.99 us -> 3.73 us  [swap(): return lax.ppermute(x, GROUP, [(i, i ^ distance) for i in range(count)])]
    pallas_call x1 -> x2, Pallas kernels: 1.8 us -> 1.87 us  [the longest x1 1.61 us: small_group(): pl.pallas_call(lambda *refs: pair_kernel([d for d, _ in last], count, nar...]
  transfers between devices with their start and end apart: 9 -> 9, of which waited for: 5 -> 5; matrix products, arithmetic and copies ran while one was open for 1% -> 1% of each run, Pallas kernels for 0% -> 1%
where the time goes in v5:
time: 19.3 us; the launch traced here: 19.1 us
  starting transfers between devices  9.53 us (49%)
  waiting for transfers between devices  4.74 us (25%)
  Pallas kernels  2.71 us (14%)
  between operations  1.98 us (10%)
    ppermute x3, starting transfers between devices, move(): return lax.ppermute(blocks, GROUP, pairs)  5.67 us
    ppermute x6, starting transfers between devices, swap(): return lax.ppermute(x, GROUP, [(i, i ^ distance) for i in range(count)])  3.86 us
    ppermute x6, waiting for transfers between devices, swap(): return lax.ppermute(x, GROUP, [(i, i ^ distance) for i in range(count)])  3.73 us
    pallas_call x1, Pallas kernels, small_group(): pl.pallas_call(lambda *refs: pair_kernel([d for d, _ in last], count, nar...  1.61 us
    ppermute x3, waiting for transfers between devices, move(): return lax.ppermute(blocks, GROUP, pairs)  1.01 us
    pallas_call x1, Pallas kernels, small_group(): pl.pallas_call(pack_kernel, out_shape=pltpu.VMEM((rows, 2 * width + LANES...  0.84 us
  transfers between devices with their start and end apart: 9, of which 5 were waited for; matrix products, arithmetic and copies ran while one was open for 1% of the time, Pallas kernels for 1%

profile of v5, /device:TPU:0, one launch (start us, length us, event | category | flops | bytes accessed | tf_op | source)
XLA Modules:
  0.0 19.1 jit_solution(11782979373123549893)
XLA Ops:
  0.6 0.8 %shard_map.79 = bf16[16,1664]{1,0:T(8,128)(2,1)S(1)} custom-call(s32[16]{0:T(128)} %mates_hbm.1, bf16[16,768]{1,0:T(8,128)(2,1)} %img_hbm.1, bf16[16,768]{1,0:T(8,128)(2,1)} %txt_hbm.1), custom_call_target="tpu_custom_call" | custom-call | tf_op jit(solution)/shard_map/pallas_call | solution.py:167
  1.5 4.1 %collective-permute-start = (bf16[16,1664]{1,0:T(8,128)(2,1)S(1)}, bf16[16,1664]{1,0:T(8,128)(2,1)S(1)}, u32[]{:S(2)}, u32[]{:S(2)}) collective-permute-start(bf16[16,1664]{1,0:T(8,128)(2,1)S(1)} %shard_map.79), channel_id=1, source_target_pairs={{12,0},{13,1},{14,2},{15,3},{8,4},{9,5},{10,6},{11,7},{0,8},{1,9},... | collective-permute-start | bytes 159752 | tf_op jit(solution)/shard_map/ppermute | solution.py:202
  5.6 1.1 %collective-permute-start.2 = (bf16[16,1664]{1,0:T(8,128)(2,1)S(1)}, bf16[16,1664]{1,0:T(8,128)(2,1)S(1)}, u32[]{:S(2)}, u32[]{:S(2)}) collective-permute-start(bf16[16,1664]{1,0:T(8,128)(2,1)S(1)} %shard_map.79), channel_id=1, source_target_pairs={{8,0},{9,1},{10,2},{11,3},{12,4},{13,5},{14,6},{15,7},{4,8},{5,9},... | collective-permute-start | bytes 159752 | tf_op jit(solution)/shard_map/ppermute | solution.py:202
  6.6 0.5 %collective-permute-start.1 = (bf16[16,1664]{1,0:T(8,128)(2,1)S(1)}, bf16[16,1664]{1,0:T(8,128)(2,1)S(1)}, u32[]{:S(2)}, u32[]{:S(2)}) collective-permute-start(bf16[16,1664]{1,0:T(8,128)(2,1)S(1)} %shard_map.79), channel_id=1, source_target_pairs={{4,0},{5,1},{6,2},{7,3},{0,4},{1,5},{2,6},{3,7},{12,8},{13,9},{14,... | collective-permute-start | bytes 159752 | tf_op jit(solution)/shard_map/ppermute | solution.py:202
  8.5 0.3 %collective-permute-done = bf16[16,1664]{1,0:T(8,128)(2,1)S(1)} collective-permute-done((bf16[16,1664]{1,0:T(8,128)(2,1)S(1)}, bf16[16,1664]{1,0:T(8,128)(2,1)S(1)}, u32[]{:S(2)}, u32[]{:S(2)}) %collective-permute-start) | collective-permute-done | bytes 53280 | tf_op jit(solution)/shard_map/ppermute | solution.py:202
  8.8 0.1 stack.6.refs_0_
  8.8 1.8 %collective-permute-start.5 = (bf16[32,1664]{1,0:T(8,128)(2,1)S(1)}, bf16[32,1664]{1,0:T(8,128)(2,1)S(1)}, u32[]{:S(2)}, u32[]{:S(2)}) collective-permute-start(bf16[32,1664]{1,0:T(8,128)(2,1)S(1)} %pad_maximum_fusion.refs_0_.refs_1_), channel_id=1, source_target_pairs={{0,2},{1,3},{2,0},{3,1},{4,6},{5,7},{6,4},{7,5},{8,10},{9,11},{10,... | collective-permute-start | bytes 319496 | tf_op jit(solution)/shard_map/ppermute | solution.py:180
  10.6 0.7 %collective-permute-done.1 = bf16[16,1664]{1,0:T(8,128)(2,1)S(1)} collective-permute-done((bf16[16,1664]{1,0:T(8,128)(2,1)S(1)}, bf16[16,1664]{1,0:T(8,128)(2,1)S(1)}, u32[]{:S(2)}, u32[]{:S(2)}) %collective-permute-start.1) | collective-permute-done | bytes 53280 | tf_op jit(solution)/shard_map/ppermute | solution.py:202
  11.3 0.0 collective-permute-done.2
  11.4 1.6 %collective-permute-start.3 = (bf16[32,1664]{1,0:T(8,128)(2,1)S(1)}, bf16[32,1664]{1,0:T(8,128)(2,1)S(1)}, u32[]{:S(2)}, u32[]{:S(2)}) collective-permute-start(bf16[32,1664]{1,0:T(8,128)(2,1)S(1)} %constant_dynamic-update-slice_fusion.refs_1_), channel_id=1, source_target_pairs={{0,2},{1,3},{2,0},{3,1},{4,6},{5,7},{6,4},{7,5},{8,10},{9,11},{10,... | collective-permute-start | bytes 319496 | tf_op jit(solution)/shard_map/ppermute | solution.py:180
  12.9 0.0 collective-permute-start.6
  12.9 0.5 %collective-permute-start.7 = (bf16[32,1664]{1,0:T(8,128)(2,1)S(1)}, bf16[32,1664]{1,0:T(8,128)(2,1)S(1)}, u32[]{:S(2)}, u32[]{:S(2)}) collective-permute-start(bf16[32,1664]{1,0:T(8,128)(2,1)S(1)} %constant_dynamic-update-slice_fusion.refs_1_), channel_id=1, source_target_pairs={{0,1},{1,0},{2,3},{3,2},{4,5},{5,4},{6,7},{7,6},{8,9},{9,8},{10,11... | collective-permute-start | bytes 319496 | tf_op jit(solution)/shard_map/ppermute | solution.py:180
  13.4 1.0 %collective-permute-done.5.refs_2_ = bf16[32,1664]{1,0:T(8,128)(2,1)S(1)} collective-permute-done((bf16[32,1664]{1,0:T(8,128)(2,1)S(1)}, bf16[32,1664]{1,0:T(8,128)(2,1)S(1)}, u32[]{:S(2)}, u32[]{:S(2)}) %collective-permute-start.5) | collective-permute-done | bytes 106528 | tf_op jit(solution)/shard_map/ppermute | solution.py:180
  14.4 0.0 collective-permute-start.8
  14.4 1.7 %collective-permute-done.3.refs_3_ = bf16[32,1664]{1,0:T(8,128)(2,1)S(1)} collective-permute-done((bf16[32,1664]{1,0:T(8,128)(2,1)S(1)}, bf16[32,1664]{1,0:T(8,128)(2,1)S(1)}, u32[]{:S(2)}, u32[]{:S(2)}) %collective-permute-start.3) | collective-permute-done | bytes 106528 | tf_op jit(solution)/shard_map/ppermute | solution.py:180
  16.1 0.0 collective-permute-start.4
  16.1 0.0 collective-permute-done.6.refs_4_
  16.1 0.0 collective-permute-done.7.refs_5_
  16.1 0.0 collective-permute-done.8.refs_6_
  16.2 0.3 %shard_map.80 = (bf16[256,768]{1,0:T(8,128)(2,1)S(1)}, bf16[256,768]{1,0:T(8,128)(2,1)S(1)}, f32[256,128]{1,0:T(8,128)S(1)}) custom-call(bf16[32,1664]{1,0:T(8,128)(2,1)S(1)} %pad_maximum_fusion.refs_0_.refs_1_, bf16[32,1664]{1,0:T(8,128)(2,1)S(1)} %constant_dynamic-update-slice_fusion.refs_1_, bf16[32,1664]{1,0:T(8,128)(2,1)S(1)} %collective-permute-done.5.refs_2_, ...), custom_call_target="tpu_custom_call" | custom-call | tf_op jit(solution)/shard_map/pallas_call | solution.py:222
  16.4 1.0 %collective-permute-done.4.refs_2_ = bf16[32,1664]{1,0:T(8,128)(2,1)S(1)} collective-permute-done((bf16[32,1664]{1,0:T(8,128)(2,1)S(1)}, bf16[32,1664]{1,0:T(8,128)(2,1)S(1)}, u32[]{:S(2)}, u32[]{:S(2)}) %collective-permute-start.4) | collective-permute-done | bytes 106528 | tf_op jit(solution)/shard_map/ppermute | solution.py:180
  17.4 1.6 %shard_map.81 = (f32[16,768]{1,0:T(8,128)}, f32[16,768]{1,0:T(8,128)}, f32[3]{0:T(128)}, bf16[256,768]{1,0:T(8,128)(2,1)S(1)}, bf16[256,768]{1,0:T(8,128)(2,1)S(1)}, /*index=5*/f32[256,128]{1,0:T(8,128)S(1)}) custom-call(f32[2,256]{1,0:T(2,128)S(1)} %stack.6.refs_0_, ...), custom_call_target="tpu_custom_call", output_to_operand_aliasing={{3}: (3, {}), {4}: (4, {}), {5}: (5, {})} | custom-call | tf_op jit(solution)/shard_map/pallas_call | solution.py:233
  (4 shorter events, 0.0 us)
Async XLA Ops:
  1.5 7.3 %collective-permute-start = (bf16[16,1664]{1,0:T(8,128)(2,1)S(1)}, bf16[16,1664]{1,0:T(8,128)(2,1)S(1)}, u32[]{:S(2)}, u32[]{:S(2)}) collective-permute-start(bf16[16,1664]{1,0:T(8,128)(2,1)S(1)} %shard_map.79), channel_id=1, source_target_pairs={{12,0},{13,1},{14,2},{15,3},{8,4},{9,5},{10,6},{11,7},{0,8},{1,9},... | collective-permute-start | bytes 159752 | tf_op jit(solution)/shard_map/ppermute | solution.py:202
  5.6 5.8 %collective-permute-start.2 = (bf16[16,1664]{1,0:T(8,128)(2,1)S(1)}, bf16[16,1664]{1,0:T(8,128)(2,1)S(1)}, u32[]{:S(2)}, u32[]{:S(2)}) collective-permute-start(bf16[16,1664]{1,0:T(8,128)(2,1)S(1)} %shard_map.79), channel_id=1, source_target_pairs={{8,0},{9,1},{10,2},{11,3},{12,4},{13,5},{14,6},{15,7},{4,8},{5,9},... | collective-permute-start | bytes 159752 | tf_op jit(solution)/shard_map/ppermute | solution.py:202
  6.6 4.7 %collective-permute-start.1 = (bf16[16,1664]{1,0:T(8,128)(2,1)S(1)}, bf16[16,1664]{1,0:T(8,128)(2,1)S(1)}, u32[]{:S(2)}, u32[]{:S(2)}) collective-permute-start(bf16[16,1664]{1,0:T(8,128)(2,1)S(1)} %shard_map.79), channel_id=1, source_target_pairs={{4,0},{5,1},{6,2},{7,3},{0,4},{1,5},{2,6},{3,7},{12,8},{13,9},{14,... | collective-permute-start | bytes 159752 | tf_op jit(solution)/shard_map/ppermute | solution.py:202
  8.8 5.6 %collective-permute-start.5 = (bf16[32,1664]{1,0:T(8,128)(2,1)S(1)}, bf16[32,1664]{1,0:T(8,128)(2,1)S(1)}, u32[]{:S(2)}, u32[]{:S(2)}) collective-permute-start(bf16[32,1664]{1,0:T(8,128)(2,1)S(1)} %pad_maximum_fusion.refs_0_.refs_1_), channel_id=1, source_target_pairs={{0,2},{1,3},{2,0},{3,1},{4,6},{5,7},{6,4},{7,5},{8,10},{9,11},{10,... | collective-permute-start | bytes 319496 | tf_op jit(solution)/shard_map/ppermute | solution.py:180
  11.4 4.8 %collective-permute-start.3 = (bf16[32,1664]{1,0:T(8,128)(2,1)S(1)}, bf16[32,1664]{1,0:T(8,128)(2,1)S(1)}, u32[]{:S(2)}, u32[]{:S(2)}) collective-permute-start(bf16[32,1664]{1,0:T(8,128)(2,1)S(1)} %constant_dynamic-update-slice_fusion.refs_1_), channel_id=1, source_target_pairs={{0,2},{1,3},{2,0},{3,1},{4,6},{5,7},{6,4},{7,5},{8,10},{9,11},{10,... | collective-permute-start | bytes 319496 | tf_op jit(solution)/shard_map/ppermute | solution.py:180
  12.9 3.2 %collective-permute-start.6 = (bf16[32,1664]{1,0:T(8,128)(2,1)S(1)}, bf16[32,1664]{1,0:T(8,128)(2,1)S(1)}, u32[]{:S(2)}, u32[]{:S(2)}) collective-permute-start(bf16[32,1664]{1,0:T(8,128)(2,1)S(1)} %pad_maximum_fusion.refs_0_.refs_1_), channel_id=1, source_target_pairs={{0,1},{1,0},{2,3},{3,2},{4,5},{5,4},{6,7},{7,6},{8,9},{9,8},{10,11... | collective-permute-start | bytes 319496 | tf_op jit(solution)/shard_map/ppermute | solution.py:180
  12.9 3.2 %collective-permute-start.7 = (bf16[32,1664]{1,0:T(8,128)(2,1)S(1)}, bf16[32,1664]{1,0:T(8,128)(2,1)S(1)}, u32[]{:S(2)}, u32[]{:S(2)}) collective-permute-start(bf16[32,1664]{1,0:T(8,128)(2,1)S(1)} %constant_dynamic-update-slice_fusion.refs_1_), channel_id=1, source_target_pairs={{0,1},{1,0},{2,3},{3,2},{4,5},{5,4},{6,7},{7,6},{8,9},{9,8},{10,11... | collective-permute-start | bytes 319496 | tf_op jit(solution)/shard_map/ppermute | solution.py:180
  14.4 1.8 %collective-permute-start.8 = (bf16[32,1664]{1,0:T(8,128)(2,1)S(1)}, bf16[32,1664]{1,0:T(8,128)(2,1)S(1)}, u32[]{:S(2)}, u32[]{:S(2)}) collective-permute-start(bf16[32,1664]{1,0:T(8,128)(2,1)S(1)} %collective-permute-done.5.refs_2_), channel_id=1, source_target_pairs={{0,1},{1,0},{2,3},{3,2},{4,5},{5,4},{6,7},{7,6},{8,9},{9,8},{10,11... | collective-permute-start | bytes 319496 | tf_op jit(solution)/shard_map/ppermute | solution.py:180
  16.1 1.3 %collective-permute-start.4 = (bf16[32,1664]{1,0:T(8,128)(2,1)S(1)}, bf16[32,1664]{1,0:T(8,128)(2,1)S(1)}, u32[]{:S(2)}, u32[]{:S(2)}) collective-permute-start(bf16[32,1664]{1,0:T(8,128)(2,1)S(1)} %collective-permute-done.3.refs_3_), channel_id=1, source_target_pairs={{0,1},{1,0},{2,3},{3,2},{4,5},{5,4},{6,7},{7,6},{8,9},{9,8},{10,11... | collective-permute-start | bytes 319496 | tf_op jit(solution)/shard_map/ppermute | solution.py:180

commit v6 on v5

--- a/solution.py
+++ b/solution.py
@@ -58,18 +58,14 @@
         copy.wait()
 
 
-def unit_rows(block, tiles):
+def own_rows(units, scales, tiles):
     parts = []
-    for first in (0, tiles):
-        values = [
-            block[0 : block.shape[0] // 2, (first + t) * LANES : (first + t + 1) * LANES].astype(jnp.float32)
-            for t in range(tiles)
+    for i in range(2):
+        first = i * tiles
+        parts += [
+            [units[:, (first + t) * LANES : (first + t + 1) * LANES] for t in range(tiles)],
+            scales[:, i * LANES : (i + 1) * LANES],
         ]
-        squares = values[0] * values[0]
-        for v in values[1:]:
-            squares = squares + v * v
-        scales = lax.rsqrt(jnp.sum(squares, axis=1, keepdims=True) + 1e-06)
-        parts += [[v * scales for v in values], scales]
     return parts
 
 
@@ -101,10 +97,17 @@
 
 def early_kernel(held, narrow, rows, width, *refs):
     me = lax.axis_index("wide") * narrow + lax.axis_index("narrow")
-    place_blocks(held, refs[: len(held)], *refs[len(held) :], me, rows, width // LANES)
-
-
-def pair_kernel(held, count, narrow, scalars_ref, own_ref, *refs):
+    buffers, (units, scales) = refs[len(held) : len(held) + 3], refs[len(held) + 3 :]
+    tiles = width // LANES
+    own = place_blocks(held, refs[: len(held)], *buffers, me, rows, tiles)
+    for i in range(2):
+        for t in range(tiles):
+            at = i * tiles + t
+            units[:, at * LANES : (at + 1) * LANES] = own[2 * i][t]
+        scales[:, i * LANES : (i + 1) * LANES] = jnp.broadcast_to(own[2 * i + 1], (rows, LANES))
+
+
+def pair_kernel(held, count, narrow, scalars_ref, units_ref, scales_ref, *refs):
     stacks, refs = refs[: len(held)], refs[len(held) + 3 :]
     image_out, text_out, summary_out, img_half, txt_half, mates, weights = refs
     rows, width = image_out.shape
@@ -112,7 +115,7 @@
     total = rows * count
     me = lax.axis_index("wide") * narrow + lax.axis_index("narrow")
 
-    own = unit_rows(own_ref, tiles)
+    own = own_rows(units_ref, scales_ref, tiles)
     place_blocks(held, stacks, img_half, txt_half, mates, me, rows, tiles)
 
     nt = (((1,), (1,)), ((), ()))
@@ -204,30 +207,33 @@
     def across(slots, blocks):
         return [lambda me, f=f: f(me ^ core) for f in slots], swap(blocks, core)
 
-    even_from, odd_from = ((3, 2, 0, 1), (1, 0, 3, 2), (2, 3, 1, 0)), ((3, 2, 0, 1), (1, 0, 3, 2), (2, 3, 1, 0))
+    even_from, odd_from = ((3, 2, 0, 1), (1, 0, 3, 2), (2, 3, 1, 0)), ((2, 3, 0, 1), (1, 0, 3, 2), (3, 2, 1, 0))
     froms = [((e, 0), (o, 0)) for e, o in zip(even_from, odd_from)]
     own_slot = slot((stay, 0), (stay, 0))
     first = move(packed, *froms[0])
     third = move(packed, *froms[2])
     near = move(packed, *froms[1])
     early, late = jnp.concatenate([packed, first]), jnp.concatenate([near, third])
-    early, scalars = lax.optimization_barrier((early, scalars))
     pairs = [[own_slot, slot(*froms[0])], [slot(*froms[1]), slot(*froms[2])]]
     flipped = [[lambda me, f=f: f(me ^ chip) for f in p] for p in pairs]
     held = [(pairs[0], early), (pairs[1], late)]
-    held += [(flipped[0], swap(early, chip)), (flipped[1], swap(late, chip))]
+    xearly, xlate = swap(early, chip), swap(late, chip)
+    xearly, scalars = lax.optimization_barrier((xearly, scalars))
+    held += [(flipped[0], xearly), (flipped[1], xlate)]
     held += [across(*part) for part in held]
 
     early_count = len(held) - 1
-    halves = pl.pallas_call(
+    *halves, units, scales = pl.pallas_call(
         lambda *refs: early_kernel([d for d, _ in held[:-1]], narrow, rows, width, *refs),
         out_shape=(
             pltpu.VMEM((total, width), jnp.bfloat16),
             pltpu.VMEM((total, width), jnp.bfloat16),
             pltpu.VMEM((total, LANES), jnp.float32),
+            pltpu.VMEM((rows, 2 * width), jnp.float32),
+            pltpu.VMEM((rows, 2 * LANES), jnp.float32),
         ),
         in_specs=[VMEM] * early_count,
-        out_specs=(VMEM, VMEM, VMEM),
+        out_specs=(VMEM,) * 5,
     )(*[in_vmem(part) for _, part in held[:-1]])
     last = held[-1:]
     return pl.pallas_call(
@@ -240,12 +246,12 @@
             pltpu.VMEM((total, width), jnp.bfloat16),
             pltpu.VMEM((total, LANES), jnp.float32),
         ),
-        in_specs=[VMEM] * 6,
+        in_specs=[VMEM] * 7,
         out_specs=(VMEM, VMEM, SMEM, VMEM, VMEM, VMEM),
-        input_output_aliases={3: 3, 4: 4, 5: 5},
+        input_output_aliases={4: 3, 5: 4, 6: 5},
         scratch_shapes=[pltpu.VMEM((total, total), jnp.bfloat16)],
         compiler_params=pltpu.CompilerParams(vmem_limit_bytes=32 * 1024 * 1024),
-    )(scalars, in_vmem(held[0][1]), last[0][1], *[in_vmem(h) for h in halves])[:3]
+    )(scalars, in_vmem(units), in_vmem(scales), last[0][1], *[in_vmem(h) for h in halves])[:3]
 
 
 def any_group(wide, narrow, images, texts, mates, sharpness, offset):

time: 19.3 us -> 19.2 us (level)
    ppermute x6, waiting for transfers between devices: 3.73 us -> 2.22 us  [swap(): return lax.ppermute(x, GROUP, [(i, i ^ distance) for i in range(count)])]
    ppermute x3, waiting for transfers between devices: 1.01 us -> 2.37 us  [move(): return lax.ppermute(blocks, GROUP, pairs)]
  transfers between devices with their start and end apart: 9 -> 9, of which waited for: 5 -> 4; matrix products, arithmetic and copies ran while one was open for 1% -> 1% of each run, Pallas kernels for 1% -> 1%
where the time goes in v6:
time: 19.2 us; the launch traced here: 19 us
  starting transfers between devices  9.65 us (50%)
  waiting for transfers between devices  4.59 us (24%)
  Pallas kernels  2.71 us (14%)
  between operations  1.98 us (10%)
    ppermute x3, starting transfers between devices, move(): return lax.ppermute(blocks, GROUP, pairs)  5.67 us
    ppermute x6, starting transfers between devices, swap(): return lax.ppermute(x, GROUP, [(i, i ^ distance) for i in range(count)])  3.99 us
    ppermute x3, waiting for transfers between devices, move(): return lax.ppermute(blocks, GROUP, pairs)  2.37 us
    ppermute x6, waiting for transfers between devices, swap(): return lax.ppermute(x, GROUP, [(i, i ^ distance) for i in range(count)])  2.22 us
    pallas_call x1, Pallas kernels, small_group(): pl.pallas_call(lambda *refs: pair_kernel([d for d, _ in last], count, nar...  1.61 us
    pallas_call x1, Pallas kernels, small_group(): pl.pallas_call(pack_kernel, out_shape=pltpu.VMEM((rows, 2 * width + LANES...  0.84 us
  transfers between devices with their start and end apart: 9, of which 4 were waited for; matrix products, arithmetic and copies ran while one was open for 1% of the time, Pallas kernels for 1%

profile of v6, /device:TPU:0, one launch (start us, length us, event | category | flops | bytes accessed | tf_op | source)
XLA Modules:
  0.0 19.0 jit_solution(8579181688992086475)
XLA Ops:
  0.6 0.8 %shard_map.79 = bf16[16,1664]{1,0:T(8,128)(2,1)S(1)} custom-call(s32[16]{0:T(128)} %mates_hbm.1, bf16[16,768]{1,0:T(8,128)(2,1)} %img_hbm.1, bf16[16,768]{1,0:T(8,128)(2,1)} %txt_hbm.1), custom_call_target="tpu_custom_call" | custom-call | tf_op jit(solution)/shard_map/pallas_call | solution.py:170
  1.5 4.1 %collective-permute-start = (bf16[16,1664]{1,0:T(8,128)(2,1)S(1)}, bf16[16,1664]{1,0:T(8,128)(2,1)S(1)}, u32[]{:S(2)}, u32[]{:S(2)}) collective-permute-start(bf16[16,1664]{1,0:T(8,128)(2,1)S(1)} %shard_map.79), channel_id=1, source_target_pairs={{12,0},{9,1},{14,2},{11,3},{8,4},{13,5},{10,6},{15,7},{0,8},{1,9},... | collective-permute-start | bytes 159752 | tf_op jit(solution)/shard_map/ppermute | solution.py:205
  5.6 1.1 %collective-permute-start.3 = (bf16[16,1664]{1,0:T(8,128)(2,1)S(1)}, bf16[16,1664]{1,0:T(8,128)(2,1)S(1)}, u32[]{:S(2)}, u32[]{:S(2)}) collective-permute-start(bf16[16,1664]{1,0:T(8,128)(2,1)S(1)} %shard_map.79), channel_id=1, source_target_pairs={{8,0},{13,1},{10,2},{15,3},{12,4},{9,5},{14,6},{11,7},{4,8},{5,9},... | collective-permute-start | bytes 159752 | tf_op jit(solution)/shard_map/ppermute | solution.py:205
  6.6 0.5 %collective-permute-start.2 = (bf16[16,1664]{1,0:T(8,128)(2,1)S(1)}, bf16[16,1664]{1,0:T(8,128)(2,1)S(1)}, u32[]{:S(2)}, u32[]{:S(2)}) collective-permute-start(bf16[16,1664]{1,0:T(8,128)(2,1)S(1)} %shard_map.79), channel_id=1, source_target_pairs={{4,0},{5,1},{6,2},{7,3},{0,4},{1,5},{2,6},{3,7},{12,8},{13,9},{14,... | collective-permute-start | bytes 159752 | tf_op jit(solution)/shard_map/ppermute | solution.py:205
  7.1 1.6 %collective-permute-done = bf16[16,1664]{1,0:T(8,128)(2,1)S(1)} collective-permute-done((bf16[16,1664]{1,0:T(8,128)(2,1)S(1)}, bf16[16,1664]{1,0:T(8,128)(2,1)S(1)}, u32[]{:S(2)}, u32[]{:S(2)}) %collective-permute-start) | collective-permute-done | bytes 53280 | tf_op jit(solution)/shard_map/ppermute | solution.py:205
  8.8 1.8 %collective-permute-start.1 = (bf16[32,1664]{1,0:T(8,128)(2,1)S(1)}, bf16[32,1664]{1,0:T(8,128)(2,1)S(1)}, u32[]{:S(2)}, u32[]{:S(2)}) collective-permute-start(bf16[32,1664]{1,0:T(8,128)(2,1)S(1)} %pad_maximum_fusion.refs_0_), channel_id=1, source_target_pairs={{0,2},{1,3},{2,0},{3,1},{4,6},{5,7},{6,4},{7,5},{8,10},{9,11},{10,... | collective-permute-start | bytes 319496 | tf_op jit(solution)/shard_map/ppermute | solution.py:183
  10.5 0.8 %collective-permute-done.2 = bf16[16,1664]{1,0:T(8,128)(2,1)S(1)} collective-permute-done((bf16[16,1664]{1,0:T(8,128)(2,1)S(1)}, bf16[16,1664]{1,0:T(8,128)(2,1)S(1)}, u32[]{:S(2)}, u32[]{:S(2)}) %collective-permute-start.2) | collective-permute-done | bytes 53280 | tf_op jit(solution)/shard_map/ppermute | solution.py:205
  11.3 0.0 collective-permute-done.3
  11.3 1.6 %collective-permute-start.4 = (bf16[32,1664]{1,0:T(8,128)(2,1)S(1)}, bf16[32,1664]{1,0:T(8,128)(2,1)S(1)}, u32[]{:S(2)}, u32[]{:S(2)}) collective-permute-start(bf16[32,1664]{1,0:T(8,128)(2,1)S(1)} %constant_dynamic-update-slice_fusion.refs_1_), channel_id=1, source_target_pairs={{0,2},{1,3},{2,0},{3,1},{4,6},{5,7},{6,4},{7,5},{8,10},{9,11},{10,... | collective-permute-start | bytes 319496 | tf_op jit(solution)/shard_map/ppermute | solution.py:183
  14.2 0.1 collective-permute-start.5
  14.3 0.5 %collective-permute-start.6 = (bf16[32,1664]{1,0:T(8,128)(2,1)S(1)}, bf16[32,1664]{1,0:T(8,128)(2,1)S(1)}, u32[]{:S(2)}, u32[]{:S(2)}) collective-permute-start(bf16[32,1664]{1,0:T(8,128)(2,1)S(1)} %constant_dynamic-update-slice_fusion.refs_1_), channel_id=1, source_target_pairs={{0,1},{1,0},{2,3},{3,2},{4,5},{5,4},{6,7},{7,6},{8,9},{9,8},{10,11... | collective-permute-start | bytes 319496 | tf_op jit(solution)/shard_map/ppermute | solution.py:183
  14.8 0.0 collective-permute-done.1.refs_2_
  14.8 0.1 stack.6.refs_0_
  14.9 0.1 collective-permute-start.7
  14.9 1.2 %collective-permute-done.4.refs_3_ = bf16[32,1664]{1,0:T(8,128)(2,1)S(1)} collective-permute-done((bf16[32,1664]{1,0:T(8,128)(2,1)S(1)}, bf16[32,1664]{1,0:T(8,128)(2,1)S(1)}, u32[]{:S(2)}, u32[]{:S(2)}) %collective-permute-start.4) | collective-permute-done | bytes 106528 | tf_op jit(solution)/shard_map/ppermute | solution.py:183
  16.1 0.0 collective-permute-start.8
  16.1 0.0 collective-permute-done.5.refs_4_
  16.1 0.0 collective-permute-done.6.refs_5_
  16.1 0.0 collective-permute-done.7.refs_6_
  16.2 0.3 %shard_map.80 = (bf16[256,768]{1,0:T(8,128)(2,1)S(1)}, bf16[256,768]{1,0:T(8,128)(2,1)S(1)}, f32[256,128]{1,0:T(8,128)S(1)}, f32[16,1536]{1,0:T(8,128)S(1)}, f32[16,256]{1,0:T(8,128)S(1)}) custom-call(bf16[32,1664]{1,0:T(8,128)(2,1)S(1)} %pad_maximum_fusion.refs_0_, bf16[32,1664]{1,0:T(8,128)(2,1)S(1)} %constant_dynamic-update-slice_fusion.refs_1_, ...), custom_call_target="tpu_custom_call" | custom-call | tf_op jit(solution)/shard_map/pallas_call | solution.py:226
  16.4 1.0 %collective-permute-done.8.refs_3_ = bf16[32,1664]{1,0:T(8,128)(2,1)S(1)} collective-permute-done((bf16[32,1664]{1,0:T(8,128)(2,1)S(1)}, bf16[32,1664]{1,0:T(8,128)(2,1)S(1)}, u32[]{:S(2)}, u32[]{:S(2)}) %collective-permute-start.8) | collective-permute-done | bytes 106528 | tf_op jit(solution)/shard_map/ppermute | solution.py:183
  17.4 1.6 %shard_map.81 = (f32[16,768]{1,0:T(8,128)}, f32[16,768]{1,0:T(8,128)}, f32[3]{0:T(128)}, bf16[256,768]{1,0:T(8,128)(2,1)S(1)}, bf16[256,768]{1,0:T(8,128)(2,1)S(1)}, /*index=5*/f32[256,128]{1,0:T(8,128)S(1)}) custom-call(f32[2,256]{1,0:T(2,128)S(1)} %stack.6.refs_0_, ...), custom_call_target="tpu_custom_call", output_to_operand_aliasing={{3}: (4, {}), {4}: (5, {}), {5}: (6, {})} | custom-call | tf_op jit(solution)/shard_map/pallas_call | solution.py:239
  (4 shorter events, 0.0 us)
Async XLA Ops:
  1.5 7.3 %collective-permute-start = (bf16[16,1664]{1,0:T(8,128)(2,1)S(1)}, bf16[16,1664]{1,0:T(8,128)(2,1)S(1)}, u32[]{:S(2)}, u32[]{:S(2)}) collective-permute-start(bf16[16,1664]{1,0:T(8,128)(2,1)S(1)} %shard_map.79), channel_id=1, source_target_pairs={{12,0},{9,1},{14,2},{11,3},{8,4},{13,5},{10,6},{15,7},{0,8},{1,9},... | collective-permute-start | bytes 159752 | tf_op jit(solution)/shard_map/ppermute | solution.py:205
  5.6 5.8 %collective-permute-start.3 = (bf16[16,1664]{1,0:T(8,128)(2,1)S(1)}, bf16[16,1664]{1,0:T(8,128)(2,1)S(1)}, u32[]{:S(2)}, u32[]{:S(2)}) collective-permute-start(bf16[16,1664]{1,0:T(8,128)(2,1)S(1)} %shard_map.79), channel_id=1, source_target_pairs={{8,0},{13,1},{10,2},{15,3},{12,4},{9,5},{14,6},{11,7},{4,8},{5,9},... | collective-permute-start | bytes 159752 | tf_op jit(solution)/shard_map/ppermute | solution.py:205
  6.6 4.7 %collective-permute-start.2 = (bf16[16,1664]{1,0:T(8,128)(2,1)S(1)}, bf16[16,1664]{1,0:T(8,128)(2,1)S(1)}, u32[]{:S(2)}, u32[]{:S(2)}) collective-permute-start(bf16[16,1664]{1,0:T(8,128)(2,1)S(1)} %shard_map.79), channel_id=1, source_target_pairs={{4,0},{5,1},{6,2},{7,3},{0,4},{1,5},{2,6},{3,7},{12,8},{13,9},{14,... | collective-permute-start | bytes 159752 | tf_op jit(solution)/shard_map/ppermute | solution.py:205
  8.8 6.0 %collective-permute-start.1 = (bf16[32,1664]{1,0:T(8,128)(2,1)S(1)}, bf16[32,1664]{1,0:T(8,128)(2,1)S(1)}, u32[]{:S(2)}, u32[]{:S(2)}) collective-permute-start(bf16[32,1664]{1,0:T(8,128)(2,1)S(1)} %pad_maximum_fusion.refs_0_), channel_id=1, source_target_pairs={{0,2},{1,3},{2,0},{3,1},{4,6},{5,7},{6,4},{7,5},{8,10},{9,11},{10,... | collective-permute-start | bytes 319496 | tf_op jit(solution)/shard_map/ppermute | solution.py:183
  11.3 4.8 %collective-permute-start.4 = (bf16[32,1664]{1,0:T(8,128)(2,1)S(1)}, bf16[32,1664]{1,0:T(8,128)(2,1)S(1)}, u32[]{:S(2)}, u32[]{:S(2)}) collective-permute-start(bf16[32,1664]{1,0:T(8,128)(2,1)S(1)} %constant_dynamic-update-slice_fusion.refs_1_), channel_id=1, source_target_pairs={{0,2},{1,3},{2,0},{3,1},{4,6},{5,7},{6,4},{7,5},{8,10},{9,11},{10,... | collective-permute-start | bytes 319496 | tf_op jit(solution)/shard_map/ppermute | solution.py:183
  14.2 1.9 %collective-permute-start.5 = (bf16[32,1664]{1,0:T(8,128)(2,1)S(1)}, bf16[32,1664]{1,0:T(8,128)(2,1)S(1)}, u32[]{:S(2)}, u32[]{:S(2)}) collective-permute-start(bf16[32,1664]{1,0:T(8,128)(2,1)S(1)} %pad_maximum_fusion.refs_0_), channel_id=1, source_target_pairs={{0,1},{1,0},{2,3},{3,2},{4,5},{5,4},{6,7},{7,6},{8,9},{9,8},{10,11... | collective-permute-start | bytes 319496 | tf_op jit(solution)/shard_map/ppermute | solution.py:183
  14.3 1.8 %collective-permute-start.6 = (bf16[32,1664]{1,0:T(8,128)(2,1)S(1)}, bf16[32,1664]{1,0:T(8,128)(2,1)S(1)}, u32[]{:S(2)}, u32[]{:S(2)}) collective-permute-start(bf16[32,1664]{1,0:T(8,128)(2,1)S(1)} %constant_dynamic-update-slice_fusion.refs_1_), channel_id=1, source_target_pairs={{0,1},{1,0},{2,3},{3,2},{4,5},{5,4},{6,7},{7,6},{8,9},{9,8},{10,11... | collective-permute-start | bytes 319496 | tf_op jit(solution)/shard_map/ppermute | solution.py:183
  14.9 1.3 %collective-permute-start.7 = (bf16[32,1664]{1,0:T(8,128)(2,1)S(1)}, bf16[32,1664]{1,0:T(8,128)(2,1)S(1)}, u32[]{:S(2)}, u32[]{:S(2)}) collective-permute-start(bf16[32,1664]{1,0:T(8,128)(2,1)S(1)} %collective-permute-done.1.refs_2_), channel_id=1, source_target_pairs={{0,1},{1,0},{2,3},{3,2},{4,5},{5,4},{6,7},{7,6},{8,9},{9,8},{10,11... | collective-permute-start | bytes 319496 | tf_op jit(solution)/shard_map/ppermute | solution.py:183
  16.1 1.3 %collective-permute-start.8 = (bf16[32,1664]{1,0:T(8,128)(2,1)S(1)}, bf16[32,1664]{1,0:T(8,128)(2,1)S(1)}, u32[]{:S(2)}, u32[]{:S(2)}) collective-permute-start(bf16[32,1664]{1,0:T(8,128)(2,1)S(1)} %collective-permute-done.4.refs_3_), channel_id=1, source_target_pairs={{0,1},{1,0},{2,3},{3,2},{4,5},{5,4},{6,7},{7,6},{8,9},{9,8},{10,11... | collective-permute-start | bytes 319496 | tf_op jit(solution)/shard_map/ppermute | solution.py:183
